TPU v7x, 128 devices: a whole 4x4x4 slice. The times are simulated.
128 devices in a mesh: ctx: 4 (over z), fsdp: 32 (over y, x, core).
Axes of the slice: x: 4, y: 4, z: 4, core: 2. Of those that a mesh axis runs over, the one named last changes fastest.
Arguments:
- tokens: bfloat16 [32, 512, 1024], P('fsdp', 'ctx'), may hold values from -6 to 6
- segments: int32 [32, 512], P('fsdp'), may hold values from 0 to 4, as said below
- cotangent: bfloat16 [32, 512, 1024], P('fsdp', 'ctx'), may hold values from -6 to 6
- gain_in: float32 [1024], P(('ctx', 'fsdp')), may hold values from 0.5 to 1.5
- mamba_in: float32 [1024, 3072], P(('ctx', 'fsdp')), may hold values from -0.1875 to 0.1875
- mamba_bc: float32 [1024, 256], P(('ctx', 'fsdp')), may hold values from -0.1875 to 0.1875
- mamba_step: float32 [1024, 24], P(('ctx', 'fsdp')), may hold values from -0.1875 to 0.1875
- in_query: float32 [1024, 512], P(('ctx', 'fsdp')), may hold values from -0.1875 to 0.1875
- in_key: float32 [1024, 128], P(('ctx', 'fsdp')), may hold values from -0.1875 to 0.1875
- in_value: float32 [1024, 128], P(('ctx', 'fsdp')), may hold values from -0.1875 to 0.1875
- mamba_out: float32 [1536, 1024], P(('ctx', 'fsdp')), may hold values from -0.15625 to 0.15625
- attn_out: float32 [512, 1024], P(('ctx', 'fsdp')), may hold values from -1 to 1
- gain_mid: float32 [1024], P(('ctx', 'fsdp')), may hold values from 0.5 to 1.5
- ffn_gate: float32 [1024, 2048], P(('ctx', 'fsdp')), may hold values from -0.1875 to 0.1875
- ffn_up: float32 [1024, 2048], P(('ctx', 'fsdp')), may hold values from -0.1875 to 0.1875
- ffn_down: float32 [2048, 1024], P(('ctx', 'fsdp')), may hold values from -0.125 to 0.125
- conv_taps: float32 [4, 1792], replicated, may hold values from -0.5 to 0.5
- conv_bias: float32 [1792], replicated, may hold values from -0.5 to 0.5
- step_bias: float32 [24], replicated, may hold values from -1 to 1
- decay_log: float32 [24], replicated, may hold values from -6.9 to -2.8
- skip_gain: float32 [24], replicated, may hold values from 0.5 to 1.5
Outputs:
- output: bfloat16 [32, 512, 1024], P('fsdp', 'ctx')
- grad_tokens: bfloat16 [32, 512, 1024], P('fsdp', 'ctx')
- grad_gain_in: float32 [1024], P(('ctx', 'fsdp'))
- grad_mamba_in: float32 [1024, 3072], P(('ctx', 'fsdp'))
- grad_mamba_bc: float32 [1024, 256], P(('ctx', 'fsdp'))
- grad_mamba_step: float32 [1024, 24], P(('ctx', 'fsdp'))
- grad_query: float32 [1024, 512], P(('ctx', 'fsdp'))
- grad_key: float32 [1024, 128], P(('ctx', 'fsdp'))
- grad_value: float32 [1024, 128], P(('ctx', 'fsdp'))
- grad_mamba_out: float32 [1536, 1024], P(('ctx', 'fsdp'))
- grad_attn_out: float32 [512, 1024], P(('ctx', 'fsdp'))
- grad_gain_mid: float32 [1024], P(('ctx', 'fsdp'))
- grad_ffn_gate: float32 [1024, 2048], P(('ctx', 'fsdp'))
- grad_ffn_up: float32 [1024, 2048], P(('ctx', 'fsdp'))
- grad_ffn_down: float32 [2048, 1024], P(('ctx', 'fsdp'))
- grad_conv_taps: float32 [4, 1792], replicated
- grad_conv_bias: float32 [1792], replicated
- grad_step_bias: float32 [24], replicated
- grad_decay_log: float32 [24], replicated
- grad_skip_gain: float32 [24], replicated
Inputs may be any that keep to these rules, and one draw needn't show every extreme that they name: `segments`: document numbers never fall along a sequence; each sequence holds five documents, one of which has positions in every block of 128.
All inputs are finite; a program needn't handle non-finite values.
Results may differ from a plain program's by a relative error of at most 0.018.
Values may be sent and summed in bfloat16 or wider, within the bound.
A program may use at most 192 MiB of HBM per device.

v0:
```python
import jax
import jax.numpy as jnp
from jax import lax
from jax.sharding import PartitionSpec as P

SSM_HEADS = 24
SSM_HEAD = 64
STATE = 128
CONV = 4
Q_HEADS = 8
KV_HEADS = 2
HEAD_DIM = 64
SPAN = 128
SSM_WIDTH = 1536


eps = 1e-06
rope_base = 100000000000.0
highest = lax.Precision.HIGHEST


def from_behind(block, axis, distance):
    devices = range(lax.axis_size(axis))
    route = [(i - distance, i) for i in devices if i - distance in devices]
    return lax.ppermute(block, axis, route)


def prefix(shard, axis, combine, identity):
    length, place = (lax.axis_size(axis), lax.axis_index(axis))
    everything = jax.tree.map(
        lambda part, kind: lax.all_gather(part.astype(kind), axis),
        shard,
        (jnp.bfloat16, jnp.bfloat16),
    )
    start = jax.tree.map(
        lambda part, zero: jnp.broadcast_to(jnp.asarray(zero, part.dtype), part.shape),
        shard,
        identity,
    )

    def step(k, before):
        reached = k < place
        new = combine(
            before, jax.tree.map(lambda part, own: part[k].astype(own.dtype), everything, shard)
        )
        return jax.tree.map(lambda a, b: jnp.where(reached, a, b), new, before)

    return lax.fori_loop(0, length, step, start)


def carried_in(shard, axis, join, neutral):
    count = lax.axis_size(axis)
    place = lax.axis_index(axis)
    ahead = count - 1 - place
    gathered = jax.tree.map(
        lambda a, kind: lax.all_gather(a.astype(kind), axis),
        shard,
        jax.tree.map(lambda a: jnp.bfloat16 if a.dtype == jnp.float32 else a.dtype, shard),
    )
    state = jax.tree.map(lambda a, e: jnp.zeros_like(a) + jnp.asarray(e, a.dtype), shard, neutral)

    def one(step, state):
        source = count - 1 - step
        return join(
            state,
            jax.tree.map(
                lambda a, own: lax.dynamic_index_in_dim(a, source, 0, False).astype(own.dtype),
                gathered,
                shard,
            ),
        )

    return lax.fori_loop(0, ahead, one, state)


def forward_dot(left_side, right_side):
    return jnp.dot(left_side, right_side, preferred_element_type=jnp.float32)


def input_grad(grad_rows, weight):
    return lax.dot_general(
        grad_rows, weight, (((1,), (1,)), ((), ())), preferred_element_type=jnp.float32
    )


def weight_grad(input_rows, grad_rows):
    return lax.dot_general(
        input_rows, grad_rows, (((0,), (0,)), ((), ())), preferred_element_type=jnp.float32
    )


def rms_scale(values, scales):
    return values * lax.rsqrt(jnp.mean(values * values, axis=-1, keepdims=True) + eps) * scales


def rotate(values, positions):
    half_dim = values.shape[-1] // 2
    frequency = rope_base ** (-2.0 * jnp.arange(half_dim, dtype=jnp.float32) / values.shape[-1])
    angles = positions.astype(jnp.float32)[:, None] * frequency[None, :]
    cosine = jnp.cos(angles)[:, None, :]
    sine_part = jnp.sin(angles)[:, None, :]
    front_part = values[..., :half_dim]
    back_part = values[..., half_dim:]
    return jnp.concatenate(
        [front_part * cosine - back_part * sine_part, front_part * sine_part + back_part * cosine],
        axis=-1,
    )


def score_block(query_block, keys, block_seg, block_pos, key_seg, scale_factor):
    scores = (
        jnp.einsum("qcgd,kcd->cgqk", query_block, keys, preferred_element_type=jnp.float32)
        * scale_factor
    )
    key_pos = jnp.arange(keys.shape[0], dtype=jnp.int32)
    allowed = (block_seg[:, None] == key_seg[None, :]) & (key_pos[None, :] <= block_pos[:, None])
    scores = jnp.where(allowed[None, None], scores, -1e30)
    shifted = jnp.exp(scores - jnp.max(scores, axis=-1, keepdims=True))
    return shifted / jnp.sum(shifted, axis=-1, keepdims=True)


def attend_forward(queries, keys, values, query_seg, key_seg, query_pos):
    row_count = queries.shape[0]
    kv_heads = keys.shape[1]
    group_size = queries.shape[1] // kv_heads
    grouped = queries.reshape(row_count, kv_heads, group_size, queries.shape[2])
    block_rows = min(row_count, 512)
    scale_factor = queries.shape[2] ** (-0.5)

    def one_block(start_row):
        probs = score_block(grouped, keys, query_seg, query_pos, key_seg, scale_factor).astype(
            jnp.bfloat16
        )
        result = jnp.einsum("cgqk,kcd->qcgd", probs, values, preferred_element_type=jnp.float32)
        return result.reshape(block_rows, -1)

    start_rows = jnp.arange(row_count // block_rows, dtype=jnp.int32) * block_rows
    return lax.map(one_block, start_rows).reshape(row_count, -1)


def attend_backward(queries, keys, values, grad_heads, query_seg, key_seg, query_pos):
    row_count = queries.shape[0]
    kv_heads = keys.shape[1]
    head_size = queries.shape[2]
    group_size = queries.shape[1] // kv_heads
    grouped = queries.reshape(row_count, kv_heads, group_size, head_size)
    grad_grouped = grad_heads.reshape(row_count, kv_heads, group_size, head_size)
    block_rows = min(row_count, 512)
    scale_factor = head_size ** (-0.5)

    def one_block(carry, start_row):
        key_total, value_total = carry
        probs = score_block(grouped, keys, query_seg, query_pos, key_seg, scale_factor)
        grad_probs = jnp.einsum(
            "qcgd,kcd->cgqk", grad_grouped, values, preferred_element_type=jnp.float32
        )
        grad_scores = probs * (grad_probs - jnp.sum(probs * grad_probs, axis=-1, keepdims=True))
        score_low = grad_scores.astype(jnp.bfloat16)
        grad_query = scale_factor * jnp.einsum(
            "cgqk,kcd->qcgd", score_low, keys, preferred_element_type=jnp.float32
        )
        key_total = key_total + scale_factor * jnp.einsum(
            "cgqk,qcgd->kcd", score_low, grouped, preferred_element_type=jnp.float32
        )
        value_total = value_total + jnp.einsum(
            "cgqk,qcgd->kcd",
            probs.astype(jnp.bfloat16),
            grad_grouped,
            preferred_element_type=jnp.float32,
        )
        return ((key_total, value_total), grad_query.reshape(block_rows, -1))

    start_rows = jnp.arange(row_count // block_rows, dtype=jnp.int32) * block_rows
    empty = jnp.zeros(keys.shape, jnp.float32)
    totals, grad_query = lax.scan(one_block, (empty, empty), start_rows)
    return (grad_query.reshape(row_count, -1), totals[0], totals[1])


def conv_rows(extended, ext_seg, row_seg, conv_taps, conv_bias):
    row_count = row_seg.shape[0]
    kernel = conv_taps.shape[0]
    total = jnp.zeros((row_count, extended.shape[1]), extended.dtype) + conv_bias[None, :]
    for tap_index in range(kernel):
        offset = kernel - 1 - tap_index
        same_doc = (ext_seg[offset : offset + row_count] == row_seg).astype(extended.dtype)
        total = (
            total
            + conv_taps[tap_index][None, :]
            * extended[offset : offset + row_count]
            * same_doc[:, None]
        )
    return jax.nn.silu(total)


def span_parts(heads_x, write_rows, read_rows, step_size, log_decay, span_seg, seg_before):
    size_rows = heads_x.shape[0]
    running = jnp.cumsum(log_decay, axis=0)
    order = jnp.arange(size_rows, dtype=jnp.int32)
    same_doc = (span_seg[:, None] == span_seg[None, :]) & (order[None, :] <= order[:, None])
    spread = running[:, None, :] - running[None, :, :]
    mixing = jnp.exp(jnp.where(same_doc[:, :, None], spread, -10000.0))
    intersection = jnp.dot(read_rows, write_rows.T, precision=highest)
    weights = mixing * intersection[:, :, None] * step_size[None, :, :]
    intra = jnp.einsum("tsh,shp->thp", weights, heads_x, precision=highest)
    inlet = (span_seg == seg_before).astype(heads_x.dtype)[:, None] * jnp.exp(running)
    tail = (
        (span_seg == span_seg[-1]).astype(heads_x.dtype)[:, None]
        * jnp.exp(running[-1][None, :] - running)
        * step_size
    )
    local_end = jnp.einsum("sh,shp,sn->hpn", tail, heads_x, write_rows, precision=highest)
    factor = jnp.exp(running[-1]) * (span_seg[-1] == seg_before).astype(heads_x.dtype)
    return (intra, inlet, local_end, factor)


def chain_join(earlier, later):
    return (earlier[0] * later[0], earlier[1] * later[0][:, None, None] + later[1])


def shards(
    tokens,
    segments,
    cotangent,
    gain_in,
    mamba_in,
    mamba_bc,
    mamba_step,
    in_query,
    in_key,
    in_value,
    mamba_out,
    attn_out,
    gain_mid,
    ffn_gate,
    ffn_up,
    ffn_down,
    conv_taps,
    conv_bias,
    step_bias,
    decay_log,
    skip_gain,
):
    row_count = tokens.shape[1]
    start_row = lax.axis_index("ctx") * row_count
    inputs = tokens[0].astype(jnp.float32)
    grad_out = cotangent[0].astype(jnp.float32)
    seq_seg = segments[0]
    row_seg = lax.dynamic_slice_in_dim(seq_seg, start_row, row_count, 0)
    pad_seg = jnp.concatenate([jnp.full((CONV - 1,), -1, jnp.int32), seq_seg], 0)
    ext_seg = lax.dynamic_slice_in_dim(pad_seg, start_row, row_count + CONV - 1, 0)
    seg_before = ext_seg[CONV - 2]
    positions = start_row + jnp.arange(row_count, dtype=jnp.int32)
    kv_width = KV_HEADS * HEAD_DIM
    mixer_w = (
        lax.all_gather(gain_in.astype(jnp.bfloat16), ("ctx", "fsdp"), axis=0, tiled=True),
        lax.all_gather(mamba_in.astype(jnp.bfloat16), ("ctx", "fsdp"), axis=0, tiled=True),
        lax.all_gather(mamba_bc.astype(jnp.bfloat16), ("ctx", "fsdp"), axis=0, tiled=True),
        lax.all_gather(mamba_step.astype(jnp.bfloat16), ("ctx", "fsdp"), axis=0, tiled=True),
        lax.all_gather(in_query.astype(jnp.bfloat16), ("ctx", "fsdp"), axis=0, tiled=True),
        lax.all_gather(in_key.astype(jnp.bfloat16), ("ctx", "fsdp"), axis=0, tiled=True),
        lax.all_gather(in_value.astype(jnp.bfloat16), ("ctx", "fsdp"), axis=0, tiled=True),
        lax.all_gather(mamba_out.astype(jnp.bfloat16), ("ctx", "fsdp"), axis=0, tiled=True),
        lax.all_gather(attn_out.astype(jnp.bfloat16), ("ctx", "fsdp"), axis=0, tiled=True),
    )
    gain_one = mixer_w[0].astype(jnp.float32)
    first_norm = rms_scale(inputs, gain_one).astype(jnp.bfloat16)
    proj_zx = forward_dot(first_norm, mixer_w[1])
    proj_bc = forward_dot(first_norm, mixer_w[2])
    proj_step = forward_dot(first_norm, mixer_w[3])
    proj_query = forward_dot(first_norm, mixer_w[4]).reshape(row_count, Q_HEADS, HEAD_DIM)
    proj_key = forward_dot(first_norm, mixer_w[5]).reshape(row_count, KV_HEADS, HEAD_DIM)
    proj_value = forward_dot(first_norm, mixer_w[6])
    raw_rows = jnp.concatenate([proj_zx[:, SSM_WIDTH:], proj_bc], axis=1).astype(jnp.bfloat16)
    gate_z = proj_zx[:, :SSM_WIDTH]
    rim_rows = from_behind(raw_rows[row_count - (CONV - 1) :], "ctx", 1)
    queries = rotate(proj_query, positions).astype(jnp.bfloat16)
    keys = rotate(proj_key, positions).astype(jnp.bfloat16).reshape(row_count, kv_width)
    values = proj_value.astype(jnp.bfloat16)
    key_all, value_all = (
        lax.all_gather(keys, "ctx", axis=0, tiled=True),
        lax.all_gather(values, "ctx", axis=0, tiled=True),
    )
    key_heads = key_all.reshape(-1, KV_HEADS, HEAD_DIM)
    value_heads = value_all.reshape(-1, KV_HEADS, HEAD_DIM)

    def front(raw_in, rim_in, drive, taps, bias, offset, decay_par):
        mixed = conv_rows(jnp.concatenate([rim_in, raw_in], 0), ext_seg, row_seg, taps, bias)
        heads_x = mixed[:, :SSM_WIDTH].reshape(row_count, SSM_HEADS, SSM_HEAD)
        write_rows = mixed[:, SSM_WIDTH : SSM_WIDTH + STATE]
        read_rows = mixed[:, SSM_WIDTH + STATE :]
        step_size = jax.nn.softplus(drive + offset)
        log_decay = -jnp.exp(decay_par) * step_size
        intra_list, inlet_list, entries, reaches = ([], [], [], [])
        entry = jnp.zeros((SSM_HEADS, SSM_HEAD, STATE), jnp.float32)
        reach = jnp.ones((SSM_HEADS,), jnp.float32)
        intra, inlet, local_end, factor = span_parts(
            heads_x, write_rows, read_rows, step_size, log_decay, row_seg, seg_before
        )
        intra_list.append(intra)
        inlet_list.append(inlet)
        entries.append(entry)
        reaches.append(reach)
        entry = factor[:, None, None] * entry + local_end
        reach = factor * reach
        return (
            jnp.concatenate(intra_list, 0),
            jnp.concatenate(inlet_list, 0),
            read_rows,
            heads_x,
            jnp.stack(entries),
            jnp.stack(reaches),
            reach,
            entry,
        )

    front_out, front_pull = jax.vjp(
        front,
        raw_rows.astype(jnp.float32),
        rim_rows.astype(jnp.float32),
        proj_step,
        conv_taps,
        conv_bias,
        step_bias,
        decay_log,
    )
    total_decay = front_out[6]
    total_state = front_out[7]
    identity = (
        jnp.ones((SSM_HEADS,), jnp.float32),
        jnp.zeros((SSM_HEADS, SSM_HEAD, STATE), jnp.float32),
    )
    incoming = prefix((total_decay, total_state), "ctx", chain_join, identity)[1]

    def finish(intra, inlet, read_rows, heads_x, entries, reaches, state_in, gate_in, skip):
        upper = SPAN
        state = reaches[0][:, None, None] * state_in + entries[0]
        pieces = [
            intra[0:upper]
            + inlet[0:upper][:, :, None]
            * jnp.einsum("tn,hpn->thp", read_rows, state, precision=highest)
        ]
        ssm_rows = jnp.concatenate(pieces, 0) + skip[None, :, None] * heads_x
        return ssm_rows.reshape(row_count, SSM_WIDTH) * jax.nn.silu(gate_in)

    gated, finish_pull = jax.vjp(
        finish,
        front_out[0],
        front_out[1],
        front_out[2],
        front_out[3],
        front_out[4],
        front_out[5],
        incoming,
        gate_z,
        skip_gain,
    )
    gated_low = gated.astype(jnp.bfloat16)
    mamba_branch = forward_dot(gated_low, mixer_w[7])
    heads = attend_forward(queries, key_heads, value_heads, row_seg, seq_seg, positions)
    merged = heads.astype(jnp.bfloat16)
    attn_branch = forward_dot(merged, mixer_w[8])
    middle = inputs + mamba_branch + attn_branch
    ffn_w = (
        lax.all_gather(gain_mid.astype(jnp.bfloat16), ("ctx", "fsdp"), axis=0, tiled=True),
        lax.all_gather(ffn_gate.astype(jnp.bfloat16), ("ctx", "fsdp"), axis=0, tiled=True),
        lax.all_gather(ffn_up.astype(jnp.bfloat16), ("ctx", "fsdp"), axis=0, tiled=True),
        lax.all_gather(ffn_down.astype(jnp.bfloat16), ("ctx", "fsdp"), axis=0, tiled=True),
    )
    gain_two = ffn_w[0].astype(jnp.float32)
    second_norm = rms_scale(middle, gain_two).astype(jnp.bfloat16)
    gate_proj = forward_dot(second_norm, ffn_w[1])
    up_proj = forward_dot(second_norm, ffn_w[2])
    hidden = (jax.nn.silu(gate_proj) * up_proj).astype(jnp.bfloat16)
    result = middle + forward_dot(hidden, ffn_w[3])
    back_all = (
        lax.all_gather(mamba_in.astype(jnp.bfloat16), ("ctx", "fsdp"), axis=0, tiled=True),
        lax.all_gather(mamba_bc.astype(jnp.bfloat16), ("ctx", "fsdp"), axis=0, tiled=True),
        lax.all_gather(mamba_step.astype(jnp.bfloat16), ("ctx", "fsdp"), axis=0, tiled=True),
        lax.all_gather(in_query.astype(jnp.bfloat16), ("ctx", "fsdp"), axis=0, tiled=True),
        lax.all_gather(in_key.astype(jnp.bfloat16), ("ctx", "fsdp"), axis=0, tiled=True),
        lax.all_gather(in_value.astype(jnp.bfloat16), ("ctx", "fsdp"), axis=0, tiled=True),
        lax.all_gather(mamba_out.astype(jnp.bfloat16), ("ctx", "fsdp"), axis=0, tiled=True),
        lax.all_gather(attn_out.astype(jnp.bfloat16), ("ctx", "fsdp"), axis=0, tiled=True),
        lax.all_gather(ffn_gate.astype(jnp.bfloat16), ("ctx", "fsdp"), axis=0, tiled=True),
        lax.all_gather(ffn_up.astype(jnp.bfloat16), ("ctx", "fsdp"), axis=0, tiled=True),
        lax.all_gather(ffn_down.astype(jnp.bfloat16), ("ctx", "fsdp"), axis=0, tiled=True),
    )
    back_mixer = back_all[:8]
    back_gate, back_up, back_down = (back_all[8], back_all[9], back_all[10])
    grad_low = grad_out.astype(jnp.bfloat16)
    grad_hidden = input_grad(grad_low, back_down)

    def swish_product(gate_in, up_in):
        return jax.nn.silu(gate_in) * up_in

    unused_swish, swish_pull = jax.vjp(swish_product, gate_proj, up_proj)
    grad_gate_f, grad_up_f = swish_pull(grad_hidden)
    grad_gate_low = grad_gate_f.astype(jnp.bfloat16)
    grad_up_low = grad_up_f.astype(jnp.bfloat16)
    grad_second = input_grad(grad_gate_low, back_gate) + input_grad(grad_up_low, back_up)
    unused_norm, second_pull = jax.vjp(rms_scale, middle, gain_two)
    grad_middle_norm, grad_gain_two = second_pull(grad_second)
    grad_middle = grad_out + grad_middle_norm
    ffn_parts = (
        lax.psum_scatter(
            weight_grad(second_norm, grad_gate_low),
            ("ctx", "fsdp"),
            scatter_dimension=0,
            tiled=True,
        ),
        lax.psum_scatter(
            weight_grad(second_norm, grad_up_low), ("ctx", "fsdp"), scatter_dimension=0, tiled=True
        ),
        lax.psum_scatter(
            weight_grad(hidden, grad_low), ("ctx", "fsdp"), scatter_dimension=0, tiled=True
        ),
    )
    grad_branch = grad_middle.astype(jnp.bfloat16)
    grad_gated = input_grad(grad_branch, back_mixer[6])
    grad_merged = input_grad(grad_branch, back_mixer[7]).astype(jnp.bfloat16)
    grad_queries, grad_keys_all, grad_values_all = attend_backward(
        queries, key_heads, value_heads, grad_merged, row_seg, seq_seg, positions
    )
    length = grad_keys_all.shape[0]
    key_grads = lax.psum_scatter(
        jnp.concatenate(
            [grad_keys_all.reshape(length, kv_width), grad_values_all.reshape(length, kv_width)],
            axis=1,
        ).astype(jnp.bfloat16),
        "ctx",
        scatter_dimension=0,
        tiled=True,
    ).astype(jnp.float32)
    grad_query_low = (
        rotate(grad_queries.reshape(row_count, Q_HEADS, HEAD_DIM), -positions)
        .reshape(row_count, -1)
        .astype(jnp.bfloat16)
    )
    grad_key_low = (
        rotate(key_grads[:, :kv_width].reshape(row_count, KV_HEADS, HEAD_DIM), -positions)
        .reshape(row_count, -1)
        .astype(jnp.bfloat16)
    )
    grad_value_low = key_grads[:, kv_width:].astype(jnp.bfloat16)
    finish_grads = finish_pull(grad_gated)
    grad_incoming = finish_grads[6]
    outgoing = carried_in((total_decay, grad_incoming), "ctx", chain_join, identity)[1]
    grad_total_decay = jnp.sum(outgoing * incoming, axis=(1, 2))
    front_grads = front_pull(
        (
            finish_grads[0],
            finish_grads[1],
            finish_grads[2],
            finish_grads[3],
            finish_grads[4],
            finish_grads[5],
            grad_total_decay,
            outgoing,
        )
    )
    grad_spill = from_behind(front_grads[1], "ctx", -1)
    grad_raw = front_grads[0].at[row_count - (CONV - 1) :].add(grad_spill)
    grad_zx_low = jnp.concatenate([finish_grads[7], grad_raw[:, :SSM_WIDTH]], axis=1).astype(
        jnp.bfloat16
    )
    grad_bc_low = grad_raw[:, SSM_WIDTH:].astype(jnp.bfloat16)
    grad_step_low = front_grads[2].astype(jnp.bfloat16)
    grad_first = (
        input_grad(grad_zx_low, back_mixer[0])
        + input_grad(grad_bc_low, back_mixer[1])
        + input_grad(grad_step_low, back_mixer[2])
        + input_grad(grad_query_low, back_mixer[3])
        + input_grad(grad_key_low, back_mixer[4])
        + input_grad(grad_value_low, back_mixer[5])
    )
    unused_first, first_pull = jax.vjp(rms_scale, inputs, gain_one)
    grad_inputs_norm, grad_gain_one = first_pull(grad_first)
    grad_tokens = (grad_middle + grad_inputs_norm).astype(jnp.bfloat16)
    mixer_parts = (
        lax.psum_scatter(
            weight_grad(first_norm, grad_zx_low), ("ctx", "fsdp"), scatter_dimension=0, tiled=True
        ),
        lax.psum_scatter(
            weight_grad(first_norm, grad_bc_low), ("ctx", "fsdp"), scatter_dimension=0, tiled=True
        ),
        lax.psum_scatter(
            weight_grad(first_norm, grad_step_low), ("ctx", "fsdp"), scatter_dimension=0, tiled=True
        ),
        lax.psum_scatter(
            weight_grad(first_norm, grad_query_low),
            ("ctx", "fsdp"),
            scatter_dimension=0,
            tiled=True,
        ),
        lax.psum_scatter(
            weight_grad(first_norm, grad_key_low), ("ctx", "fsdp"), scatter_dimension=0, tiled=True
        ),
        lax.psum_scatter(
            weight_grad(first_norm, grad_value_low),
            ("ctx", "fsdp"),
            scatter_dimension=0,
            tiled=True,
        ),
        lax.psum_scatter(
            weight_grad(gated_low, grad_branch), ("ctx", "fsdp"), scatter_dimension=0, tiled=True
        ),
        lax.psum_scatter(
            weight_grad(merged, grad_branch), ("ctx", "fsdp"), scatter_dimension=0, tiled=True
        ),
    )
    weight_parts = tuple(mixer_parts) + tuple(ffn_parts)
    small_parts = lax.psum(
        (
            front_grads[3],
            front_grads[4],
            front_grads[5],
            front_grads[6],
            finish_grads[8],
            grad_gain_one,
            grad_gain_two,
        ),
        ("ctx", "fsdp"),
    )
    shard_len = gain_in.shape[0]
    flat_index = lax.axis_index("ctx") * lax.axis_size("fsdp") + lax.axis_index("fsdp")
    gain_one_part = lax.dynamic_slice_in_dim(small_parts[5], flat_index * shard_len, shard_len, 0)
    gain_two_part = lax.dynamic_slice_in_dim(small_parts[6], flat_index * shard_len, shard_len, 0)
    return (
        result.astype(jnp.bfloat16)[None],
        grad_tokens[None],
        gain_one_part,
        weight_parts[0],
        weight_parts[1],
        weight_parts[2],
        weight_parts[3],
        weight_parts[4],
        weight_parts[5],
        weight_parts[6],
        weight_parts[7],
        gain_two_part,
        weight_parts[8],
        weight_parts[9],
        weight_parts[10],
        small_parts[0],
        small_parts[1],
        small_parts[2],
        small_parts[3],
        small_parts[4],
    )


def solution(mesh):
    return jax.shard_map(
        shards,
        mesh=mesh,
        in_specs=(
            P("fsdp", "ctx", None),
            P("fsdp", None),
            P("fsdp", "ctx", None),
            P(("ctx", "fsdp")),
            P(("ctx", "fsdp"), None),
            P(("ctx", "fsdp"), None),
            P(("ctx", "fsdp"), None),
            P(("ctx", "fsdp"), None),
            P(("ctx", "fsdp"), None),
            P(("ctx", "fsdp"), None),
            P(("ctx", "fsdp"), None),
            P(("ctx", "fsdp"), None),
            P(("ctx", "fsdp")),
            P(("ctx", "fsdp"), None),
            P(("ctx", "fsdp"), None),
            P(("ctx", "fsdp"), None),
            P(),
            P(),
            P(),
            P(),
            P(),
        ),
        out_specs=(
            P("fsdp", "ctx", None),
            P("fsdp", "ctx", None),
            P(("ctx", "fsdp")),
            P(("ctx", "fsdp"), None),
            P(("ctx", "fsdp"), None),
            P(("ctx", "fsdp"), None),
            P(("ctx", "fsdp"), None),
            P(("ctx", "fsdp"), None),
            P(("ctx", "fsdp"), None),
            P(("ctx", "fsdp"), None),
            P(("ctx", "fsdp"), None),
            P(("ctx", "fsdp")),
            P(("ctx", "fsdp"), None),
            P(("ctx", "fsdp"), None),
            P(("ctx", "fsdp"), None),
            P(),
            P(),
            P(),
            P(),
            P(),
        ),
        check_vma=False,
    )
```

profile of v0, /device:TPU:1, one launch (start us, length us, event | category | flops | bytes accessed | tf_op | source)
XLA Modules:
  0.0 4202.2 jit_solution(17443827434691125900)
XLA Ops:
  18.2 69.3 %all-reduce.24 = (bf16[1024]{0:T(1024)(128)(2,1)S(1)}, bf16[1024]{0:T(1024)(128)(2,1)S(1)}) all-reduce(bf16[1024]{0:T(1024)(128)(2,1)S(1)} %dynamic-update-slice.3, bf16[1024]{0:T(1024)(128)(2,1)S(1)} %dynamic-update-slice.4), channel_id=1, replica_groups=mesh['ctx'=4,'fsdp'=32] {'ctx','fsdp'}, use_global_device_ids=true, to_apply=%add.14 | all-reduce | flops 2048 | bytes 8192
  88.8 34.3 all_gather.77
  130.9 33.8 all_gather.76
  165.9 3.8 fusion.171
  178.3 7.8 all-gather.2
  186.1 36.4 all_gather.84
  222.7 33.3 all_gather.82
  256.3 9.1 all_gather.83
  266.1 9.9 all_gather.85
  286.6 6.2 reshape.624
  293.9 12.7 all-gather.25.cloned.1.call-done
  306.6 4.9 while.40
  313.8 4.1 fusion.26
  325.5 51.9 %all-gather.19.cloned.1.call-done = bf16[1024,2048]{1,0:T(8,128)(2,1)} async-done(((bf16[8,2048]{1,0:T(8,128)(2,1)}), bf16[1024,2048]{1,0:T(8,128)(2,1)}) %all-gather.19.cloned.1.call-update) | async-done | bytes 4194320 | tf_op jit(solution)/shard_map/all_gather | solution.py:365
  377.4 3.9 fusion.178
  381.3 64.2 %all-gather.21.cloned.1.call-done = bf16[1024,2048]{1,0:T(8,128)(2,1)} async-done(((bf16[8,2048]{1,0:T(8,128)(2,1)}), bf16[1024,2048]{1,0:T(8,128)(2,1)}) %all-gather.21.cloned.1.call-update) | async-done | bytes 4194320 | tf_op jit(solution)/shard_map/all_gather | solution.py:366
  445.5 3.9 fusion.179
  449.4 63.6 %all-gather.23.cloned.1.call-done = bf16[2048,1024]{1,0:T(8,128)(2,1)} async-done(((bf16[16,1024]{1,0:T(8,128)(2,1)}), bf16[2048,1024]{1,0:T(8,128)(2,1)}) %all-gather.23.cloned.1.call-update) | async-done | bytes 4194320 | tf_op jit(solution)/shard_map/all_gather | solution.py:367
  513.0 5.5 multiply_convert_fusion
  535.0 5.6 multiply_reduce_fusion.6
  549.0 5.1 fusion.45
  558.2 22.8 all-gather.27.cloned.1.call-done
  581.1 5.8 while.19
  612.4 4.0 fusion.20
  621.5 3.8 multiply_reduce_fusion.4
  632.8 4.5 fusion.184
  638.4 4.6 fusion.185
  644.1 4.5 fusion.96
  649.7 6.5 fusion.88
  657.2 3.6 fusion.182
  660.9 375.6 %fusion = f32[16,1024]{1,0:T(8,128)S(1)} fusion(f32[1536,1024]{1,0:T(8,128)} %fusion.182), kind=kCustom, calls=%all-reduce-scatter | all-reduce-scatter fusion | flops 2097153 | bytes 6356992
  1046.9 11.3 collective-permute-start.17
  1058.3 10.0 collective-permute-start.18
  1068.3 4.2 collective-permute-start.19
  1074.6 3.9 collective-permute-start.20
  1098.7 4.0 collective-permute-start.30
  1109.1 3.8 collective-permute-start.5
  1120.7 4.4 collective-permute-start.9
  1125.1 3.6 fusion.33
  1129.1 50.7 %concatenate.50 = f32[524,1024]{1,0:T(8,128)} concatenate(f32[12,1024]{1,0:T(8,128)} %copy-done.79, f32[16,1024]{1,0:T(8,128)} %collective-permute-done.32, f32[16,1024]{1,0:T(8,128)} %collective-permute-done.31, f32[16,1024]{1,0:T(8,128)} %collective-permute-done.30, f32[16,1024]{1,0:T(8,128)} %copy-done.99, f32[16,1024]{1,0:T(8,128)} %copy-done.98, f32[16,1024]{1,0:T(8,128)} %copy-done.97, ...), dimensions={0} | concatenate | bytes 4292608
  1182.0 5.1 fusion.89
  1189.1 62.9 %all-reduce.22 = (f32[1024]{0:T(1024)S(1)}, f32[1024]{0:T(1024)S(1)}, f32[4,1792]{1,0:T(4,128)}, f32[1792]{0:T(1024)}, f32[24]{0:T(128)}, /*index=5*/f32[24]{0:T(128)}, f32[24]{0:T(128)}) all-reduce(f32[1024]{0:T(1024)S(1)} %get-tuple-element.298, f32[1024]{0:T(1024)S(1)} %copy-done.117, ...), channel_id=1, replica_groups=mesh['ctx'=4,'fsdp'=32] {'ctx','fsdp'}, use_global_device_ids=true, to_apply=%region_23.24 | all-reduce | flops 11080 | bytes 88640 | tf_op jit(solution)/shard_map/psum | solution.py:512
  1259.4 134.2 %reduce-scatter.16.cloned.1.call-done = f32[8,512]{1,0:T(8,128)} async-done(((f32[1024,512]{1,0:T(8,128)}), f32[8,512]{1,0:T(8,128)}) %reduce-scatter.16.cloned.1.call-update) | async-done | bytes 16400 | tf_op jit(solution)/shard_map/reduce_scatter | solution.py:489
  1393.5 635.6 %reduce-scatter.14.cloned.1.call-done = f32[8,256]{1,0:T(8,128)} async-done(((f32[1024,256]{1,0:T(8,128)}), f32[8,256]{1,0:T(8,128)}) %reduce-scatter.14.cloned.1.call-update) | async-done | bytes 8208 | tf_op jit(solution)/shard_map/reduce_scatter | solution.py:483
  2029.1 646.8 %reduce-scatter.18.cloned.1.call-done = f32[8,2048]{1,0:T(8,128)} async-done(((f32[1024,2048]{1,0:T(8,128)}), f32[8,2048]{1,0:T(8,128)}) %reduce-scatter.18.cloned.1.call-update) | async-done | bytes 65552 | tf_op jit(solution)/shard_map/reduce_scatter | solution.py:405
  2675.9 646.7 %reduce-scatter.20.cloned.1.call-done = f32[8,2048]{1,0:T(8,128)} async-done(((f32[1024,2048]{1,0:T(8,128)}), f32[8,2048]{1,0:T(8,128)}) %reduce-scatter.20.cloned.1.call-update) | async-done | bytes 65552 | tf_op jit(solution)/shard_map/reduce_scatter | solution.py:411
  3322.6 646.8 %reduce-scatter.22.cloned.1.call-done = f32[16,1024]{1,0:T(8,128)} async-done(((f32[2048,1024]{1,0:T(8,128)}), f32[16,1024]{1,0:T(8,128)}) %reduce-scatter.22.cloned.1.call-update) | async-done | bytes 65552 | tf_op jit(solution)/shard_map/reduce_scatter | solution.py:414
  3969.4 225.9 %reduce-scatter.12.cloned.1.call-done = f32[8,3072]{1,0:T(8,128)} async-done(((f32[1024,3072]{1,0:T(8,128)}), f32[8,3072]{1,0:T(8,128)}) %reduce-scatter.12.cloned.1.call-update) | async-done | bytes 98320 | tf_op jit(solution)/shard_map/reduce_scatter | solution.py:480
  (573 shorter events, 189.5 us)
Async XLA Ops:
  7.2 158.7 %all-gather.15.cloned.1.call-start = ((), (), s32[]{:S(2)}) async-start(), calls=%async_computation.7 | async-start | bytes 6340608 | tf_op jit(solution)/shard_map/all_gather | solution.py:256
  8.8 268.1 %all-gather.17.cloned.1.call-start = ((), (), s32[]{:S(2)}) async-start(), calls=%async_computation.8 | async-start | bytes 1056768 | tf_op jit(solution)/shard_map/all_gather | solution.py:259
  10.2 269.0 %all-gather.31.cloned.1.call-start = ((), (), s32[]{:S(2)}) async-start(), calls=%async_computation.21 | async-start | bytes 1056768 | tf_op jit(solution)/shard_map/all_gather | solution.py:263
  11.6 275.0 %all-gather.29.cloned.1.call-start = ((), (), s32[]{:S(2)}) async-start(), calls=%async_computation.20 | async-start | bytes 4227072 | tf_op jit(solution)/shard_map/all_gather | solution.py:262
  13.1 293.4 %all-gather.25.cloned.1.call-start = ((), (), s32[]{:S(2)}) async-start(), calls=%async_computation.18 | async-start | bytes 1966080 | tf_op jit(solution)/shard_map/all_gather | solution.py:31
  175.9 201.6 %all-gather.19.cloned.1.call-start = ((), (), s32[]{:S(2)}) async-start(), calls=%async_computation.9 | async-start | bytes 4227072 | tf_op jit(solution)/shard_map/all_gather | solution.py:365
  176.6 269.0 %all-gather.21.cloned.1.call-start = ((), (), s32[]{:S(2)}) async-start(), calls=%async_computation.10 | async-start | bytes 4227072 | tf_op jit(solution)/shard_map/all_gather | solution.py:366
  177.3 335.7 %all-gather.23.cloned.1.call-start = ((), (), s32[]{:S(2)}) async-start(), calls=%async_computation.11 | async-start | bytes 4227072 | tf_op jit(solution)/shard_map/all_gather | solution.py:367
  178.1 376.1 %reduce-scatter.24.cloned.1.call-start = ((), (), s32[]{:S(2)}) async-start(), calls=%async_computation.22 | async-start | bytes 327680
  534.9 46.1 %all-gather.27.cloned.1.call-start = ((), (), s32[]{:S(2)}) async-start(), calls=%async_computation.19 | async-start | bytes 1966080 | tf_op jit(solution)/shard_map/all_gather | solution.py:56
  544.3 709.8 %all-reduce.27.cloned.1.call-start = ((), (), s32[]{:S(2)}) async-start(), calls=%async_computation.23 | async-start | bytes 7340032
  604.7 788.8 %reduce-scatter.16.cloned.1.call-start = ((), (), s32[]{:S(2)}) async-start(), calls=%async_computation.14 | async-start | bytes 2113536 | tf_op jit(solution)/shard_map/reduce_scatter | solution.py:489
  609.0 1420.1 %reduce-scatter.14.cloned.1.call-start = ((), (), s32[]{:S(2)}) async-start(), calls=%async_computation.13 | async-start | bytes 1056768 | tf_op jit(solution)/shard_map/reduce_scatter | solution.py:483
  632.7 2043.2 %reduce-scatter.18.cloned.1.call-start = ((), (), s32[]{:S(2)}) async-start(), calls=%async_computation.15 | async-start | bytes 8454144 | tf_op jit(solution)/shard_map/reduce_scatter | solution.py:405
  637.4 2685.2 %reduce-scatter.20.cloned.1.call-start = ((), (), s32[]{:S(2)}) async-start(), calls=%async_computation.16 | async-start | bytes 8454144 | tf_op jit(solution)/shard_map/reduce_scatter | solution.py:411
  643.0 3326.3 %reduce-scatter.22.cloned.1.call-start = ((), (), s32[]{:S(2)}) async-start(), calls=%async_computation.17 | async-start | bytes 8454144 | tf_op jit(solution)/shard_map/reduce_scatter | solution.py:414
  648.7 3546.6 %reduce-scatter.12.cloned.1.call-start = ((), (), s32[]{:S(2)}) async-start(), calls=%async_computation.12 | async-start | bytes 12681216 | tf_op jit(solution)/shard_map/reduce_scatter | solution.py:480
  1036.4 7.8 collective-permute-start.10
  1039.1 6.6 collective-permute-start.11
  1040.4 6.6 collective-permute-start.12
  1041.7 16.6 collective-permute-start.13
  1043.0 25.3 collective-permute-start.14
  1044.3 28.3 collective-permute-start.15
  1045.6 28.9 collective-permute-start.16
  1046.9 31.5 collective-permute-start.17
  1058.3 22.0 collective-permute-start.18
  1068.3 13.5 collective-permute-start.19
  1072.6 12.7 collective-permute-start.2
  1074.6 12.1 collective-permute-start.20
  1078.4 9.5 collective-permute-start.21
  1080.2 9.0 collective-permute-start.22
  1081.9 8.9 collective-permute-start.23
  1085.3 8.8 collective-permute-start.24
  1086.6 8.8 collective-permute-start.25
  1088.0 10.8 collective-permute-start.26
  1089.3 13.5 collective-permute-start.27
  1090.8 13.9 collective-permute-start.28
  1094.2 12.4 collective-permute-start.29
  1095.5 13.6 collective-permute-start.3
  1098.7 14.2 collective-permute-start.30
  1102.8 12.1 collective-permute-start.31
  1104.7 13.1 collective-permute-start.32
  1106.6 14.1 collective-permute-start.4
  1109.1 20.0 collective-permute-start.5
  1112.9 16.1 collective-permute-start.6
  1114.8 14.3 collective-permute-start.7
  1117.8 11.3 collective-permute-start.8
  1120.7 8.4 collective-permute-start.9
  (157 other events, 4774.4 us)
Sparse Core Ops, SparseCore 0:
  11.7 71.9 all-gather.14
  87.1 61.3 all-gather.16
  151.9 61.0 all-gather.30
  216.5 64.5 all-gather.28
  282.6 23.9 all-gather.24
  310.2 67.2 all-gather.18
  381.1 64.3 all-gather.20
  448.7 64.3 all-gather.22
  535.0 15.6 reduce-scatter.23
  552.3 28.6 all-gather.26
  604.9 152.8 all-reduce.26
  760.6 632.8 reduce-scatter.15
  1396.4 632.6 reduce-scatter.13
  2032.0 643.7 reduce-scatter.17
  2678.7 643.8 reduce-scatter.19
  3325.5 643.8 reduce-scatter.21
  3974.8 220.4 reduce-scatter.11
where the time goes:
time: 4220 us; the launch traced here: 4200 us
  waiting for transfers between devices  3160 us (75%)
  blocking collectives  672 us (16%)
  matrix products  117 us (3%)
  local copies, waits for them, and re-layouts  99.8 us (2%)
  starting transfers between devices  91.6 us (2%)
  other arithmetic  46.7 us (1%)
    reduce_scatter x1, waiting for transfers between devices, shards(): lax.psum_scatter(weight_grad(hidden, grad_low), ('ctx', 'fsdp'), scatter_...  647 us
    reduce_scatter x1, waiting for transfers between devices, shards(): lax.psum_scatter(weight_grad(second_norm, grad_gate_low), ('ctx', 'fsdp')...  647 us
    reduce_scatter x1, waiting for transfers between devices, shards(): lax.psum_scatter(weight_grad(second_norm, grad_up_low), ('ctx', 'fsdp'),...  647 us
    reduce_scatter x1, waiting for transfers between devices, shards(): lax.psum_scatter(weight_grad(first_norm, grad_bc_low), ('ctx', 'fsdp'), s...  636 us
    unnamed x2, blocking collectives  445 us
    reduce_scatter x1, waiting for transfers between devices, shards(): lax.psum_scatter(weight_grad(first_norm, grad_zx_low), ('ctx', 'fsdp'), s...  226 us
    reduce_scatter x1, waiting for transfers between devices, shards(): lax.psum_scatter(weight_grad(first_norm, grad_query_low), ('ctx', 'fsdp')...  134 us
    unnamed x34, starting transfers between devices  88 us
  transfers between devices with their start and end apart: 51, of which 13 were waited for; matrix products, arithmetic and copies ran while one was open for 14% of the time, Pallas kernels for 0%

commit v1 on v0

v1 whole, which is shorter than its diff:
```python
import types

import jax
import jax.numpy as jnp
import numpy as np
from jax import lax
from jax.experimental import pallas as pl
from jax.experimental.pallas import tpu as pltpu
from jax.sharding import PartitionSpec as P

BF = jnp.bfloat16
F32 = jnp.float32
MESH = pl.DeviceIdType.MESH
HI = lax.Precision.HIGHEST
EPS = 1e-06
ROPE = 100000000000.0

D = 1024
LEN = 512
ROWS = 128
HEADS = 6
XW = 384
CW = 640
GW = 384
PK = 3584
FW = 512


def mm(a, b):
    return lax.dot_general(a, b, (((1,), (0,)), ((), ())), preferred_element_type=F32)


def mm_nt(a, b):
    return lax.dot_general(a, b, (((1,), (1,)), ((), ())), preferred_element_type=F32)


def mm_tn(a, b):
    return lax.dot_general(a, b, (((0,), (0,)), ((), ())), preferred_element_type=F32)


def mm_exact(a, b):
    return lax.dot_general(
        a, b, (((1,), (0,)), ((), ())), precision=HI, preferred_element_type=F32
    )


def iota(shape, dim):
    return lax.broadcasted_iota(jnp.int32, shape, dim)


def lane_low(shape):
    return iota(shape, 1) % 128 < 64


def roll(v, shift, axis):
    size = v.shape[axis]
    return pltpu.roll(v, shift % size, axis)


def swap_halves(v):
    lanes = v.shape[1]
    first = iota(v.shape, 1) % 64 < 32
    return jnp.where(first, roll(v, lanes - 32, 1), roll(v, 32, 1))


def sigmoid(v):
    return 1.0 / (1.0 + jnp.exp(-v))


def softplus(v):
    return jnp.maximum(v, 0.0) + jnp.log1p(jnp.exp(-jnp.abs(v)))


def spread_heads(v):
    rows = v.shape[0]
    low = lane_low((rows, 128))
    tiles = []
    for pair in range(HEADS // 2):
        a = jnp.broadcast_to(v[:, 2 * pair : 2 * pair + 1], (rows, 128))
        b = jnp.broadcast_to(v[:, 2 * pair + 1 : 2 * pair + 2], (rows, 128))
        tiles.append(jnp.where(low, a, b))
    return jnp.concatenate(tiles, axis=1)


def mm_terms(a, b, count):
    side = 0 if a.dtype == F32 else 1
    rest, total = (a, b)[side], None
    for _ in range(count):
        term = rest.astype(BF)
        rest = rest - term.astype(F32)
        one = mm(term, b) if side == 0 else mm(a, term)
        total = one if total is None else total + one
    return total


def sum_heads(v):
    pick = (iota((XW, 128), 0) // 64 == iota((XW, 128), 1)).astype(BF)
    return mm_terms(v, pick, 2)


def lower_ones():
    return (iota((ROWS, ROWS), 1) <= iota((ROWS, ROWS), 0)).astype(BF)


LATE, EARLY, OUT = (0, 2 * GW), (2 * GW, 2 * GW), (4 * GW, 512)
FIN, FOUT = (2048, 2 * FW), (2048 + 2 * FW, 512)
FFN = (FIN[0], FIN[1] + FOUT[1])


def chunk(R, core, kind, k, lo=0, width=GW):
    v = R.win[core, k // 2, :, :, :, pl.ds(kind[0] + GW * (k % 2) + lo, width)]
    return v.reshape(256, width)


def group_weight(R, core, kind):
    return jnp.concatenate([chunk(R, core, kind, k) for k in range(4)], axis=0)


def out_weight(R, kind=OUT):
    parts = []
    for core in range(2):
        rows = [R.win[core, d, :, :, :, pl.ds(kind[0], 512)].reshape(256, 512) for d in range(2)]
        parts.append(jnp.concatenate(rows, axis=0))
    return jnp.concatenate(parts, axis=1)


def seg_mask(R, k):
    seg = R.segc[...]
    return jnp.where(
        (seg == roll(seg, k, 0)) & (iota((LEN, 128), 0) >= k), 1.0, 0.0
    ).astype(F32)


def gains(R):
    pick = (iota((8, 128), 1) == iota((8, 128), 0) + 24).astype(BF)
    for k in range(4):
        R.gain[:, pl.ds(256 * k, 256)] = mm_nt(pick, chunk(R, 1, LATE, k, 256, 128))


def norm_first(R):
    gain = R.gain[0:1, :]

    def block(b, carry):
        x = R.xall[b].astype(F32)
        inv = lax.rsqrt(jnp.mean(x * x, axis=-1, keepdims=True) + EPS)
        R.first[pl.ds(pl.multiple_of(b * ROWS, ROWS), ROWS), :] = (x * inv * gain).astype(BF)
        return carry

    lax.fori_loop(0, 4, block, 0)


def project_late(R):
    first = R.first[...]
    out = mm(first, group_weight(R, 0, LATE))
    R.raw[:, 0:384] = out.astype(BF)
    out = mm(first, group_weight(R, 1, LATE))
    R.raw[:, 384:640] = out[:, 0:256].astype(BF)
    R.pm[...] = out[:, 256:384]


def project_early(R):
    first = R.first[...]
    out = mm(first, group_weight(R, 1, EARLY))
    R.pq[...] = out[:, 0:128]
    R.pkv[...] = out[:, 128:256]
    R.gate[...] = mm(first, group_weight(R, 0, EARLY))


def convolve(R):
    masks = [seg_mask(R, k) for k in range(1, 4)]
    for t in range(CW // 128):
        cols = slice(128 * t, 128 * t + 128)
        raw = R.raw[:, cols].astype(F32)
        total = R.cpar[4:5, cols] + R.cpar[0:1, cols] * raw
        for k in range(1, 4):
            total = total + R.cpar[k : k + 1, cols] * (roll(raw, k, 0) * masks[k - 1])
        R.pre[:, cols] = total
        R.mixed[:, cols] = total * sigmoid(total)


def steps(R):
    step = softplus(R.pm[...] + R.hpar[0:1, :])
    R.step[...] = step
    decay = -jnp.exp(R.hpar[1:2, :])
    ones = lower_ones()
    for b in range(4):
        rows = slice(b * ROWS, b * ROWS + ROWS)
        R.run[rows, :] = mm_terms(ones, decay * step[rows, :], 3)


def span(R, b):
    s = types.SimpleNamespace()
    s.at = pl.multiple_of(b * ROWS, ROWS)
    s.rows = pl.ds(s.at, ROWS)
    s.xs = R.mixed[s.rows, 0:384]
    s.xs_low = s.xs.astype(BF)
    s.wr_low = R.mixed[s.rows, 384:512].astype(BF)
    s.rd_low = R.mixed[s.rows, 512:640].astype(BF)
    s.step = R.step[s.rows, :]
    return s


def recurrence(R, begin, end):
    low = lane_low((ROWS, 128))

    def block(b, carry):
        s = span(R, b)
        run = R.run[s.rows, :]
        run_t = run.T
        seg = R.segc[s.rows, :]
        last = jnp.broadcast_to(seg[ROWS - 1 : ROWS, :], (ROWS, ROWS))
        earlier = R.segc[pl.ds(pl.multiple_of(jnp.maximum(s.at - 8, 0), 8), 8), :][7:8, :]
        earlier = jnp.where(jnp.broadcast_to(b, (1, 128)) == 0, -1.0, earlier)
        causal = (iota((ROWS, ROWS), 1) <= iota((ROWS, ROWS), 0)) & (
            seg == R.segr[0:1, s.rows]
        )
        inlet = jnp.where(seg == earlier, jnp.exp(run), 0.0)
        stop = run[ROWS - 1 : ROWS, :]
        tail0 = jnp.where(seg == last, jnp.exp(stop - run), 0.0)
        factor = jnp.where(last[0:1, :] == earlier, jnp.exp(stop), 0.0)
        inlet_x = spread_heads(inlet)
        step_x = spread_heads(s.step)
        tail_x = spread_heads(tail0)
        xstep = step_x * s.xs
        xstep_low = xstep.astype(BF)
        factor_x = spread_heads(jnp.broadcast_to(factor, (8, 128)))
        R.step_x[s.rows, :] = step_x
        R.factor[b] = jnp.broadcast_to(factor, (8, 128))
        R.inlet_x[s.rows, :] = inlet_x
        R.tail_x[s.rows, :] = tail_x
        R.factor_x[b] = factor_x
        cross = mm_nt(s.rd_low, s.wr_low)
        state = R.state[b]
        inflow = mm(s.rd_low, state.astype(BF))
        tiles = []
        for pair in range(HEADS // 2):
            xp = xstep_low[:, 128 * pair : 128 * pair + 128]
            both = []
            for h in (2 * pair, 2 * pair + 1):
                spread = run[:, h : h + 1] - run_t[h : h + 1, :]
                mix = jnp.exp(jnp.where(causal, spread, -10000.0))
                weights = (mix * cross).astype(BF)
                R.mix[b, h] = mix.astype(BF)
                R.weights[b, h] = weights
                both.append(mm(weights, xp))
            tiles.append(jnp.where(low, both[0], both[1]))
        R.ssm[s.rows, :] = (
            jnp.concatenate(tiles, axis=1) + inlet_x * inflow + R.cpar[5:6, 0:384] * s.xs
        )
        R.state[b + 1] = factor_x[0:1, :] * state + mm_tn(
            s.wr_low, (tail_x * xstep).astype(BF)
        )
        return carry

    lax.fori_loop(begin, end, block, 0)


def rotate(v, cosr, sinr):
    return v * cosr + swap_halves(v) * sinr


def rotated(R):
    low = lane_low((LEN, 128))
    R.q[...] = rotate(R.pq[...], R.cosr[...], R.sinr[...]).astype(BF)
    pkv = R.pkv[...]
    k = rotate(pkv, R.cosr[...], R.sinr[...])
    R.kk[...] = jnp.where(low, k, roll(k, 64, 1)).astype(BF)
    R.vv[...] = jnp.where(low, roll(pkv, 64, 1), pkv).astype(BF)


def half_only(v, e):
    low = lane_low(v.shape)
    return jnp.where(low if e == 0 else ~low, v, jnp.zeros_like(v))


def attend(R, begin, end):
    low = lane_low((ROWS, 128))
    for i in range(begin, end):
        rows = slice(i * ROWS, i * ROWS + ROWS)
        n = (i + 1) * ROWS
        seg_row = R.segr[0:1, 0:n]
        seg_col = jnp.broadcast_to(R.segc[rows, 0:1], (ROWS, n))
        allowed = (iota((ROWS, n), 1) <= iota((ROWS, n), 0) + i * ROWS) & (seg_col == seg_row)
        outs = []
        for e in range(2):
            scores = mm_nt(half_only(R.q[rows, :], e), R.kk[0:n, :]) * 0.125
            scores = jnp.where(allowed, scores, -1e30)
            shifted = jnp.exp(scores - jnp.max(scores, axis=-1, keepdims=True))
            probs = (shifted / jnp.sum(shifted, axis=-1, keepdims=True)).astype(BF)
            R.probs[e, rows, 0:n] = probs
            outs.append(mm(probs, R.vv[0:n, :]))
        R.left[rows, 384:512] = jnp.where(low, outs[0], outs[1]).astype(BF)


def out_project(R, h):
    rows = slice(256 * h, 256 * h + 256)
    gate = R.gate[rows, :]
    R.left[rows, 0:384] = (R.ssm[rows, :] * (gate * sigmoid(gate))).astype(BF)
    left = mm(R.left[rows, :], R.perm5[...]).astype(BF)
    R.left_p[rows, :] = left
    out = mm(left, out_weight(R))
    for j in range(4):
        R.branch[h, j] = out[64 * j : 64 * j + 64, :].astype(BF)


def unit_chunk(R, core, k):
    lo = FIN[0] + FW * (k % 2)
    return R.win[core, k // 2, :, :, :, lo : lo + FW].reshape(256, FW)


def ffn(R, h):
    second = R.secall[h].reshape(256, D)
    cot = R.cotall[2 * h : 2 * h + 2].reshape(256, D)
    rows = slice(256 * h, 256 * h + 256)
    for d in range(2):
        cols = slice(256 * d, 256 * d + 256)
        weights = []
        for core in range(2):
            parts = [unit_chunk(R, core, k)[:, cols] for k in range(4)]
            weights.append(jnp.concatenate(parts, axis=0))
        a = mm(second, weights[0])
        b = mm(second, weights[1])
        down = jnp.concatenate(
            [R.win[core, d, :, :, :, FOUT[0] : PK].reshape(256, 512) for core in range(2)], axis=1
        )
        ghid = mm_nt(cot, down)
        sig = sigmoid(a)
        act = a * sig
        R.hid[rows, cols] = (act * b).astype(BF)
        R.gab[rows, cols] = (ghid * b * (sig + act * (1.0 - sig))).astype(BF)
        R.gab[rows, FW + 256 * d : FW + 256 * d + 256] = (ghid * act).astype(BF)
    for k in range(4):
        weights = jnp.concatenate([unit_chunk(R, core, k) for core in range(2)], axis=1)
        out = mm_nt(R.gab[rows, :], weights)
        for j in range(4):
            R.gsec[h, j, :, 256 * k : 256 * k + 256] = out[64 * j : 64 * j + 64, :].astype(BF)


def ffn_out(R, L):
    out = mm(R.hid[...], out_weight(R, FOUT))
    for b in range(4):
        R.fout[b] = out[b * ROWS : b * ROWS + ROWS, :].astype(BF)
    for h in range(2):
        block, rows = mid_rows(L, h)
        R.fout[block, rows, :] = (
            R.fout[block, rows, :].astype(F32) + R.middle[h]
        ).astype(BF)


def ffn_grads(R):
    second = R.secall[...].reshape(LEN, D)
    for k in range(4):
        out = mm_tn(second[:, 256 * k : 256 * k + 256], R.gab[...]).astype(BF)
        lo = FIN[0] + FW * (k % 2)
        for core in range(2):
            part = out[:, FW * core : FW * core + FW]
            R.win[core, k // 2, :, :, :, lo : lo + FW] = part.reshape(4, 4, 16, FW)
    put_out_grad(R.win, FOUT, mm_tn(R.hid[...], R.cotall[...].reshape(LEN, D)))


def norm_back(x, gain, grad):
    inv = lax.rsqrt(jnp.mean(x * x, axis=-1, keepdims=True) + EPS)
    unit = x * inv
    scaled = grad * gain
    return inv * (scaled - unit * jnp.mean(scaled * unit, axis=-1, keepdims=True))


def mid_rows(L, h):
    return 2 * h + lax.div(L.z, 2), pl.ds(pl.multiple_of(64 * lax.rem(L.z, 2), 64), 64)


def back_out(R, h):
    rows = slice(256 * h, 256 * h + 256)
    raw = mm_nt(R.gball[h].reshape(256, D), out_weight(R))
    perm = R.perm5[...]
    hi = raw.astype(BF)
    rest = raw - hi.astype(F32)
    R.gleft[rows, :] = mm_nt(hi, perm) + mm_nt(rest.astype(BF), perm)


def back_gate(R):
    def block(b, carry):
        rows = pl.ds(pl.multiple_of(b * ROWS, ROWS), ROWS)
        gate = R.gate[rows, :]
        sig = sigmoid(gate)
        grad = R.gleft[rows, 0:384] * R.ssm[rows, :]
        R.gproj[rows, 768:1152] = (grad * (sig + gate * sig * (1.0 - sig))).astype(BF)
        return carry

    lax.fori_loop(0, 4, block, 0)


def back_attend(R, begin, end):
    low = lane_low((ROWS, 128))
    for i in range(begin, end):
        rows = slice(i * ROWS, i * ROWS + ROWS)
        n = (i + 1) * ROWS
        go = R.gleft[rows, 384:512].astype(BF)
        outs = []
        for e in range(2):
            probs = R.probs[e, rows, 0:n]
            pf = probs.astype(F32)
            go_e = half_only(go, e)
            dp = mm_nt(go_e, R.vv[0:n, :])
            ds = (pf * (dp - jnp.sum(pf * dp, axis=-1, keepdims=True))).astype(BF)
            outs.append(mm(ds, R.kk[0:n, :]))
            R.gk[0:n, :] += mm_tn(ds, half_only(R.q[rows, :], e))
            R.gv[0:n, :] += mm_tn(probs, go_e)
        R.gq[rows, :] = jnp.where(low, outs[0], outs[1]) * 0.125


def back_rotated(R):
    cosr, sinr = R.cosr[...], R.sinr[...]
    gq = rotate(R.gq[...], cosr, -sinr)
    R.gproj[:, 1152:1280] = gq.astype(BF)
    gk = R.gk[...] * 0.125
    gk = rotate(gk + roll(gk, 64, 1), cosr, -sinr)
    gv = R.gv[...]
    gv = gv + roll(gv, 64, 1)
    R.gproj[:, 1280:1408] = jnp.where(lane_low((LEN, 128)), gk, gv).astype(BF)
    R.gproj[:, 1408:1536] = jnp.zeros((LEN, 128), BF)


def back_recurrence(R):
    R.gstate[...] = jnp.zeros((128, XW), F32)
    R.hsum[...] = jnp.zeros((8, 128), F32)
    low = lane_low((ROWS, 128))
    lane = iota((ROWS, 128), 1)
    sub = iota((ROWS, 128), 0)
    upper = (iota((ROWS, ROWS), 1) >= iota((ROWS, ROWS), 0)).astype(BF)

    def block(i, carry):
        b = 3 - i
        s = span(R, b)
        state = R.state[b]
        state_low = state.astype(BF)
        gstate = R.gstate[...]
        gstate_low = gstate.astype(BF)
        gate = R.gate[s.rows, :]
        gy = R.gleft[s.rows, 0:384] * (gate * sigmoid(gate))
        gy_low = gy.astype(BF)
        step_x = R.step_x[s.rows, :]
        tail_x = R.tail_x[s.rows, :]
        xstep = step_x * s.xs
        xstep_low = xstep.astype(BF)
        skip = R.cpar[5:6, 0:384]
        gcross = jnp.zeros((ROWS, ROWS), F32)
        tiles = []
        for pair in range(HEADS // 2):
            cols = slice(128 * pair, 128 * pair + 128)
            gp = gy_low[:, cols]
            both = []
            for e in range(2):
                h = 2 * pair + e
                both.append(mm_tn(R.weights[b, h], gp))
                gm = mm_nt(half_only(gp, e), xstep_low[:, cols])
                gcross = gcross + gm * R.mix[b, h].astype(F32)
            tiles.append(jnp.where(low, both[0], both[1]))
        inside = jnp.concatenate(tiles, axis=1)
        outflow = tail_x * mm(s.wr_low, gstate_low)
        flow_low = (R.inlet_x[s.rows, :] * gy).astype(BF)
        gcross_low = gcross.astype(BF)
        R.gmix[s.rows, 0:384] = (inside + outflow) * step_x + skip * gy
        R.gmix[s.rows, 384:512] = mm_tn(gcross_low, s.rd_low) + mm_nt(
            (tail_x * xstep).astype(BF), gstate_low
        )
        R.gmix[s.rows, 512:640] = mm(gcross_low, s.wr_low) + mm_nt(flow_low, state_low)
        ends = jnp.concatenate(
            [
                jnp.sum(gstate * state, axis=0, keepdims=True),
                jnp.sum(gy * s.xs, axis=0, keepdims=True),
                jnp.zeros((6, XW), F32),
            ],
            axis=0,
        )
        sums = sum_heads(
            jnp.concatenate(
                [
                    gy * (R.ssm[s.rows, :] - skip * s.xs),
                    inside * s.xs,
                    outflow * s.xs,
                    ends,
                ],
                axis=0,
            )
        )
        row_part = sums[0:ROWS, :]
        col_part = sums[ROWS : 2 * ROWS, :]
        through = sums[2 * ROWS : 3 * ROWS, :]
        gfactor = sums[3 * ROWS : 3 * ROWS + 1, :]
        grun = row_part - (col_part + through) * s.step
        at_end = (
            jnp.sum(through * s.step, axis=0, keepdims=True) + gfactor * R.factor[b, 0:1, :]
        )
        grun = grun + jnp.where(sub == ROWS - 1, at_end, 0.0)
        glog = mm_terms(upper, grun, 3)
        decay = -jnp.exp(R.hpar[1:2, :])
        gstep = col_part + through + glog * decay
        drive = R.pm[s.rows, :] + R.hpar[0:1, :]
        gdrive = jnp.where(lane < HEADS, gstep * sigmoid(drive), 0.0)
        R.gproj[s.rows, 640:768] = gdrive.astype(BF)
        R.hsum[0:1, :] += jnp.sum(gdrive, axis=0, keepdims=True)
        R.hsum[1:2, :] += jnp.sum(glog * decay * s.step, axis=0, keepdims=True)
        R.hsum[2:3, :] += sums[3 * ROWS + 1 : 3 * ROWS + 2, :]
        R.gstate[...] = R.factor_x[b, 0:1, :] * gstate + mm_tn(s.rd_low, flow_low)
        return carry

    lax.fori_loop(0, 4, block, 0)


def back_convolve(R):
    masks = [seg_mask(R, k) for k in range(1, 4)]
    for t in range(CW // 128):
        cols = slice(128 * t, 128 * t + 128)
        pre = R.pre[:, cols]
        raw = R.raw[:, cols].astype(F32)
        sig = sigmoid(pre)
        gpre = R.gmix[:, cols] * (sig + pre * sig * (1.0 - sig))
        graw = R.cpar[0:1, cols] * gpre
        R.small[0:1, cols] = jnp.sum(gpre * raw, axis=0, keepdims=True)
        for k in range(1, 4):
            masked = gpre * masks[k - 1]
            graw = graw + R.cpar[k : k + 1, cols] * roll(masked, LEN - k, 0)
            R.small[k : k + 1, cols] = jnp.sum(masked * roll(raw, k, 0), axis=0, keepdims=True)
        R.small[4:5, cols] = jnp.sum(gpre, axis=0, keepdims=True)
        R.gproj[:, cols] = graw.astype(BF)


def back_first(R, L):
    places = ((0, LATE), (1, LATE), (0, EARLY), (1, EARLY))
    gain = R.gain[0:1, :]
    moves = []
    for n, k in enumerate((2, 1, 3, 0)):
        b = L.around("z", k)
        rows = pl.ds(pl.multiple_of(b * ROWS, ROWS), ROWS)
        grads = R.gproj[rows, :]
        for q in range(4):
            weights = jnp.concatenate([chunk(R, core, kind, q) for core, kind in places], axis=1)
            R.gsum[:, 256 * q : 256 * q + 256] = mm_nt(grads, weights)
        R.gfirst[b] = norm_back(R.xall[b].astype(F32), gain, R.gsum[...]).astype(BF)
        for h in range(2):
            block, rows = mid_rows(L, h)

            @pl.when(block == b)
            def _():
                mine = R.gfirst[b, rows, :].astype(F32) + R.gmid[h]
                R.gfirst[b, rows, :] = mine.astype(BF)

        if k:
            moves.append(L.copy(R.gfirst.at[b], R.hrecv.at[n], L.device(z=b)))
        yield
    for one in moves:
        one.wait_recv()
    add_blocks(())(R.gfirst.at[L.z], [R.hrecv.at[n] for n in range(3)])


def put_out_grad(buf, kind, out):
    out = out.astype(BF)
    for core in range(2):
        for d in range(2):
            part = out[256 * d : 256 * d + 256, 512 * core : 512 * core + 512]
            buf[core, d, :, :, :, kind[0] : kind[0] + 512] = part.reshape(4, 4, 16, 512)


def out_grad(R):
    put_out_grad(R.dwin, OUT, mm_tn(R.left_p[...], R.gball[...].reshape(LEN, D)))


def put_grad(R, core, kind, k, value):
    lo = kind[0] + GW * (k % 2)
    R.dwin[core, k // 2, :, :, :, lo : lo + GW] = value.astype(BF).reshape(4, 4, 16, GW)


def early_grads(R):
    for k in range(4):
        out = mm_tn(R.first[:, 256 * k : 256 * k + 256], R.gproj[:, 768:1536])
        for core in range(2):
            put_grad(R, core, EARLY, k, out[:, GW * core : GW * core + GW])


def late_grads(R):
    for k in range(4):
        out = mm_tn(R.first[:, 256 * k : 256 * k + 256], R.gproj[:, 0:768])
        for core in range(2):
            put_grad(R, core, LATE, k, out[:, GW * core : GW * core + GW])


class Move:
    def __init__(self, one):
        self.one, self.came, self.went = one, False, False

    def wait_recv(self):
        if not self.came:
            self.one.wait_recv()
            self.came = True

    def wait_send(self):
        if not self.went:
            self.one.wait_send()
            self.went = True


class Links:
    def __init__(self, send, recv):
        self.send, self.recv, self.moves = send, recv, []
        self.z = lax.axis_index("ctx")
        place = lax.axis_index("fsdp")
        self.c = lax.rem(place, 2)
        self.x = lax.rem(lax.div(place, 2), 4)
        self.y = lax.div(place, 8)
        self.at = {"z": self.z, "y": self.y, "x": self.x}
        self.sibling = self.device(c=1 - self.c)

    def device(self, **moved):
        p = dict(z=self.z, y=self.y, x=self.x, c=self.c)
        p.update(moved)
        return (p["z"], (p["y"] * 4 + p["x"]) * 2 + p["c"])

    def copy(self, src, dst, device):
        k = len(self.moves)
        one = pltpu.make_async_remote_copy(
            src_ref=src,
            dst_ref=dst,
            send_sem=self.send.at[k],
            recv_sem=self.recv.at[k],
            device_id=device,
            device_id_type=MESH,
        )
        one.start()
        self.moves.append(Move(one))
        return self.moves[-1]

    def around(self, axis, k):
        return lax.rem(self.at[axis] + k, 4)

    def slab(self):
        for dz in range(4):
            for flip in range(2):
                if dz or flip:
                    yield self.around("z", dz), self.c if flip == 0 else 1 - self.c

    def greet(self):
        barrier = pltpu.get_barrier_semaphore()
        to = [self.device(z=j, c=h) for j, h in self.slab()]
        for axis in ("x", "y"):
            to += [self.device(**{axis: self.around(axis, k)}) for k in range(1, 4)]
        for one in to:
            pl.semaphore_signal(barrier, inc=1, device_id=one, device_id_type=MESH)
        return lambda: pl.semaphore_wait(barrier, len(to))

    def settle(self):
        for one in self.moves:
            one.wait_send()

    def finish(self):
        for one in self.moves:
            one.wait_recv()
            one.wait_send()


def gather(L, axis, slot, arrived=None, log=None):
    me = L.at[axis]
    moves = [
        (k, L.copy(slot(me), slot(me), L.device(**{axis: L.around(axis, k)}))) for k in (2, 1, 3)
    ]
    if log is not None:
        log.extend(one for _, one in moves)
    if arrived:
        arrived(me)
    yield
    for k, one in moves[1:] + moves[:1]:
        one.wait_recv()
        if arrived:
            arrived(L.around(axis, 4 - k))


def reduce(L, axis, src, bufs, add):
    moves = []
    for buf, k in zip(bufs, (2, 1, 3)):
        j = L.around(axis, k)
        moves.append(L.copy(src(j), buf, L.device(**{axis: j})))
    yield
    for one in moves:
        one.wait_recv()
    add(src(L.at[axis]), bufs)


def add_blocks(lead):
    count = int(np.prod(lead)) if lead else 1

    def add(dst, srcs):
        def body(n, carry):
            where = []
            for size in reversed(lead):
                where.append(lax.rem(n, size))
                n = lax.div(n, size)
            where = tuple(reversed(where)) + (slice(None), slice(None))
            total = dst[where].astype(F32)
            for one in srcs:
                total = total + one[where].astype(F32)
            dst[where] = total.astype(BF)
            return carry

        lax.fori_loop(0, count, body, 0)

    return add


def columns(ref, lead, lo, width):
    return ref.at[(slice(None),) * (lead + 1) + (pl.ds(lo, width),)]


def step(*gens):
    for g in gens:
        next(g, None)


def together(*gens):
    gens = list(gens)
    while gens:
        alive = []
        for g in gens:
            try:
                next(g)
                alive.append(g)
            except StopIteration:
                pass
        gens = alive
        if gens:
            yield


def drain(*gens):
    for _ in together(*gens):
        pass


def mixer_slot(L, buf, sub, stage, lo, width):
    ref = buf.at[L.c, sub]
    axis = ("xy" if sub == 0 else "yx")[stage]

    def slot(j):
        if stage == 0:
            block = ref.at[L.y, j] if axis == "x" else ref.at[j, L.x]
        else:
            block = ref.at[j] if axis == "y" else ref.at[:, j]
        return columns(block, stage, lo, width)

    return axis, slot


def gather_mixer(L, R, sub, lo, width, log=None):
    sent = []
    for stage in range(2):
        axis, slot = mixer_slot(L, R.win, sub, stage, lo, width)

        def arrived(j, slot=slot):
            sent.append(L.copy(slot(j), slot(j), L.sibling))

        yield from gather(L, axis, slot, arrived if stage == 1 else None, log)
    if log is not None:
        log.extend(sent)
    yield
    for one in sent:
        one.wait_recv()


def reduce_mixer(L, R, buf, lo, width):
    moves = []
    for sub in range(2):
        theirs = columns(buf.at[1 - L.c, sub], 2, lo, width)
        moves.append(L.copy(theirs, columns(R.wsib.at[sub], 2, lo, width), L.sibling))
    yield
    gens = []
    for sub in range(2):
        moves[sub].wait_recv()
        mine = columns(buf.at[L.c, sub], 2, lo, width)
        add_blocks((4, 4))(mine, [columns(R.wsib.at[sub], 2, lo, width)])
        gens.append(reduce_chips(L, R, buf, sub, lo, width))
        next(gens[-1])
    yield
    yield from together(*gens)


def reduce_chips(L, R, buf, sub, lo, width):
    for stage in (1, 0):
        axis, slot = mixer_slot(L, buf, sub, stage, lo, width)
        bufs = [columns(one.at[sub], stage, lo, width) for one in R.mbufs[stage]]
        yield from reduce(L, axis, slot, bufs, add_blocks((4,) * stage))


def deal_rows(L, buf, kind, width, fin, rfin, place):
    for sub in range(2):
        for k in range(2):
            lo = kind[0] + width * k
            both = buf[L.c, sub, L.y, L.x, :, lo : lo + width].astype(F32)
            for core in range(2):
                fin[2 * sub + k, core, :, place : place + width] = both[8 * core : 8 * core + 8, :]
    cols = pl.ds(place, width)
    moves = [
        L.copy(fin.at[j, h, :, cols], rfin.at[L.z, L.c, :, cols], L.device(z=j, c=h))
        for j, h in L.slab()
    ]
    rfin[L.z, L.c, :, cols] = fin[L.z, L.c, :, cols]
    return moves


def deal_halves(L, buf, kind, fin, rfin):
    for d in range(2):
        fin[d] = buf[L.c, d, L.y, L.x, :, kind[0] : kind[0] + 512].astype(F32)
    return L.copy(fin.at[1 - L.c], rfin, L.sibling)


def reduce_inputs(L, R, kind, place):
    yield from reduce_mixer(L, R, R.dwin, *kind)
    moves = deal_rows(L, R.dwin, kind, GW, R.fin, R.rfin, place)
    yield
    for one in moves:
        one.wait_recv()


def reduce_outputs(L, R):
    yield from reduce_mixer(L, R, R.dwin, *OUT)
    move = deal_halves(L, R.dwin, OUT, R.ofin, R.orfin)
    yield
    move.wait_recv()
    lo, hi = in_core_order(L, R.ofin[L.c], R.orfin[...])
    R.o_mo[:, 0:512] = lo[0:12, :]
    R.o_mo[:, 512:1024] = hi[0:12, :]
    R.o_ao[:, 0:512] = lo[12:16, :]
    R.o_ao[:, 512:1024] = hi[12:16, :]
    R.send_out("o_mo", "o_ao")


def reduce_ffn(L, R):
    yield from reduce_mixer(L, R, R.win, *FFN)
    moves = deal_rows(L, R.win, FIN, FW, R.ffin, R.frfin, 0)
    moves.append(deal_halves(L, R.win, FOUT, R.dfin, R.drfin))
    yield
    for one in moves:
        one.wait_recv()
    lo, hi = in_core_order(L, R.dfin[L.c], R.drfin[...])
    R.o_fd[:, 0:512] = lo
    R.o_fd[:, 512:1024] = hi
    turn = (iota((FW, FW), 1) == deal(iota((FW, FW), 0))).astype(F32)
    rows = [R.frfin[j, core] for core in range(2) for j in range(4)]
    out = mm_exact(jnp.concatenate(rows, axis=0), turn)
    for j in range(4):
        R.o_fg[:, FW * j : FW * j + FW] = out[8 * j : 8 * j + 8, :]
        R.o_fu[:, FW * j : FW * j + FW] = out[32 + 8 * j : 40 + 8 * j, :]
    R.gcol[0] = gain_column([(R.w_fg, R.o_fg), (R.w_fu, R.o_fu)], R.gain_mid)
    R.send_out("o_fd", "o_fg", "o_fu")


def reduce_blocks(L, ref, recv):
    return reduce(L, "z", lambda j: ref.at[j], [recv.at[n] for n in range(3)], add_blocks(()))


def gather_blocks(L, ref):
    return gather(L, "z", lambda j: ref.at[j])


def reduce_small(L, R):
    for part in range(3):
        R.small[5:6, 128 * part : 128 * part + 128] = R.hsum[part : part + 1, :]
    R.smc[L.c] = R.small[...]
    move = L.copy(R.smc.at[L.c], R.smc.at[L.c], L.sibling)
    yield
    move.wait_recv()
    R.smx[L.x] = R.smc[0] + R.smc[1]
    yield from gather(L, "x", lambda j: R.smx.at[j])
    R.smy[L.y] = (R.smx[0] + R.smx[1]) + (R.smx[2] + R.smx[3])
    yield from gather(L, "y", lambda j: R.smy.at[j])
    R.smz[L.z] = (R.smy[0] + R.smy[1]) + (R.smy[2] + R.smy[3])
    yield from gather(L, "z", lambda j: R.smz.at[j])
    for j in range(4):
        R.o_conv[:, 384 * j : 384 * j + 384] = R.smz[j, :, 0:384]
    total = (R.smz[0] + R.smz[1]) + (R.smz[2] + R.smz[3])
    R.o_conv[:, 1536:1792] = total[:, 384:640]
    lane = iota((8, 128), 1)
    for part in range(3):
        heads = jnp.zeros((8, 128), F32)
        for j in range(4):
            one = jnp.where(lane < HEADS, R.smz[j, :, 128 * part : 128 * part + 128], 0.0)
            heads = heads + (one if j == 0 else roll(one, HEADS * j, 1))
        R.o_head[part : part + 1, :] = heads[5:6, :]


def setup(L, R):
    lane = iota((1, 128), 1)
    first = HEADS * L.z
    for row, ref in enumerate((R.step_bias, R.decay_log)):
        total = jnp.zeros((1, 128), F32)
        for h in range(HEADS):
            total = jnp.where(lane == h, ref[first + h], total)
        R.hpar[row : row + 1, :] = total
    cols = pl.ds(pl.multiple_of(XW * L.z, 128), XW)
    R.cpar[0:4, 0:384] = R.taps[:, cols]
    R.cpar[0:4, 384:640] = R.taps[:, 1536:1792]
    R.cpar[4:5, 0:384] = R.bias[:, cols]
    R.cpar[4:5, 384:640] = R.bias[:, 1536:1792]
    lane = iota((1, XW), 1) // 64
    total = jnp.zeros((1, XW), F32)
    for h in range(HEADS):
        total = jnp.where(lane == h, R.skip_gain[first + h], total)
    R.cpar[5:6, 0:384] = total
    seg = R.seg[...].astype(F32)
    R.segr[0:1, :] = seg
    for b in range(4):
        row = seg[:, b * ROWS : b * ROWS + ROWS]
        R.segc[b * ROWS : b * ROWS + ROWS, :] = jnp.broadcast_to(row, (ROWS, ROWS)).T


def pack_weights(L, R):
    shape8 = (8, 128)
    low = lane_low(shape8)
    lane = iota(shape8, 1)
    sub = iota(shape8, 0)
    k, v = R.w_k[...], R.w_v[...]
    k_up, v_up = roll(k, 64, 1), roll(v, 64, 1)
    R.misc[...] = jnp.zeros(shape8, F32)
    R.misc[:, 0:24] = R.w_step[...]
    misc = R.misc[...]
    for row in range(8):
        misc = jnp.where((lane == 24) & (sub == row), R.gain_in[row], misc)
        misc = jnp.where((lane == 25) & (sub == row), R.gain_mid[row], misc)
    for j in range(4):
        R.pack[j, 0, :, 0:384] = R.w_min[:, 1536 + 384 * j : 1920 + 384 * j]
        R.pack[j, 0, :, 384:768] = R.w_min[:, 384 * j : 384 * j + 384]
        R.pack[j, 1, :, 0:256] = R.w_bc[...]
        mine = misc if j == 0 else roll(misc, 128 - HEADS * j, 1)
        R.pack[j, 1, :, 256:384] = jnp.where(
            lane < HEADS, mine, jnp.where((lane >= 24) & (lane < 26), misc, 0.0)
        )
        R.pack[j, 1, :, 384:512] = R.w_q[:, 128 * j : 128 * j + 128]
        R.pack[j, 1, :, 512:640] = jnp.where(low, k, v_up) if j < 2 else jnp.where(low, k_up, v)
        R.pack[j, 1, :, 640:768] = jnp.zeros(shape8, F32)
    for h in range(2):
        R.opack[h, 0:12, :] = R.w_mo[:, 512 * h : 512 * h + 512]
        R.opack[h, 12:16, :] = R.w_ao[:, 512 * h : 512 * h + 512]


def deal(n):
    return 32 * ((n % 256) // 16) + 16 * (n // 256) + n % 16


def pack_ffn(L, R):
    turn = (iota((FW, FW), 0) == deal(iota((FW, FW), 1))).astype(BF)
    rows = [ref[:, FW * j : FW * j + FW] for ref in (R.w_fg, R.w_fu) for j in range(4)]
    out = mm(jnp.concatenate(rows, axis=0).astype(BF), turn)
    for j in range(4):
        R.fpack[j, 0] = out[8 * j : 8 * j + 8, :]
        R.fpack[j, 1] = out[32 + 8 * j : 40 + 8 * j, :]
    for h in range(2):
        R.dpack[h] = R.w_fd[:, 512 * h : 512 * h + 512]


def gain_column(pairs, scalars):
    total = jnp.zeros((8, 1), F32)
    for weight, grad in pairs:
        weight = weight[...].astype(BF).astype(F32)
        total = total + jnp.sum(weight * grad[...], axis=1, keepdims=True)
    sub = iota((8, 128), 0)
    gain = jnp.ones((8, 128), F32)
    for row in range(8):
        gain = jnp.where(sub == row, scalars[row], gain)
    return total / gain.astype(BF).astype(F32)


def unpack_inputs(R):
    lane = iota((8, 128), 1)
    low = lane_low((8, 128))
    misc = jnp.zeros((8, 128), F32)
    for j in range(4):
        R.o_min[:, 384 * j : 384 * j + 384] = R.rfin[j, 0, :, 384:768]
        R.o_min[:, 1536 + 384 * j : 1920 + 384 * j] = R.rfin[j, 0, :, 0:384]
        R.o_q[:, 128 * j : 128 * j + 128] = R.rfin[j, 1, :, 384:512]
        part = R.rfin[j, 1, :, 256:384]
        own = jnp.where(lane < HEADS, part, 0.0)
        misc = misc + (own if j == 0 else roll(own, HEADS * j, 1))
    R.o_misc[...] = misc
    R.o_bc[...] = (R.rfin[0, 1, :, 0:256] + R.rfin[1, 1, :, 0:256]) + (
        R.rfin[2, 1, :, 0:256] + R.rfin[3, 1, :, 0:256]
    )
    kv0 = R.rfin[0, 1, :, 512:640] + R.rfin[1, 1, :, 512:640]
    kv1 = R.rfin[2, 1, :, 512:640] + R.rfin[3, 1, :, 512:640]
    R.o_k[...] = jnp.where(low, kv0, roll(kv1, 64, 1))
    R.o_v[...] = jnp.where(low, roll(kv0, 64, 1), kv1)
    pairs = [(R.w_min, R.o_min), (R.w_bc, R.o_bc), (R.w_step, R.o_misc.at[:, 0:24])]
    pairs += [(R.w_q, R.o_q), (R.w_k, R.o_k), (R.w_v, R.o_v)]
    first = gain_column(pairs, R.gain_in)
    both = jnp.where(iota((8, 128), 1) == 0, first, R.gcol[0])
    turned = jnp.concatenate([both, jnp.zeros((120, 128), F32)], axis=0).T
    R.o_head[3:5, :] = turned[0:2, :]


def in_core_order(L, mine, other):
    first = L.c == 0
    return jnp.where(first, mine, other), jnp.where(first, other, mine)


def own_rows(L, R, exch, kinds, width):
    for sub in range(2):
        for k in range(2):
            both = jnp.concatenate([exch[2 * sub + k, d] for d in range(2)], axis=0).astype(BF)
            for n, kind in enumerate(kinds):
                lo = kind[0] + width * k
                R.win[L.c, sub, L.y, L.x, :, lo : lo + width] = both[:, width * n : width * n + width]


def own_halves(L, R, pack, other, kind):
    for d, part in enumerate(in_core_order(L, pack[L.c], other[...])):
        R.win[L.c, d, L.y, L.x, :, kind[0] : kind[0] + 512] = part.astype(BF)


def to_slab(L, pack, exch):
    moves = [L.copy(pack.at[j, h], exch.at[L.z, L.c], L.device(z=j, c=h)) for j, h in L.slab()]
    exch[L.z, L.c] = pack[L.z, L.c]
    return moves


def come(*moves):
    for one in moves:
        one.wait_recv()


def middle_rows(L, R, h):
    block, rows = mid_rows(L, h)
    total = R.xall[block, rows, :].astype(F32) + R.branch[h, L.z].astype(F32)
    for n in range(3):
        total = total + R.zrecv[h, n].astype(F32)
    R.middle[h] = total
    inv = lax.rsqrt(jnp.mean(total * total, axis=-1, keepdims=True) + EPS)
    R.secall[h, L.z] = (total * inv * R.gain[1:2, :]).astype(BF)


def back_middle(L, R, h):
    block, rows = mid_rows(L, h)
    total = R.gsec[h, L.z].astype(F32)
    for n in range(3):
        total = total + R.zrecv[2 + h, n].astype(F32)
    gmid = norm_back(R.middle[h], R.gain[1:2, :], total)
    gmid = gmid + R.cotall[block, rows, :].astype(F32)
    R.gmid[h] = gmid
    R.gball[h, L.z] = gmid.astype(BF)


def keep(dst, srcs):
    pass


def to_owner(L, R, ref, n):
    return reduce(L, "z", lambda j: ref.at[j], [R.zrecv.at[n, k] for k in range(3)], keep)


def kernel(R):
    L = Links(R.send, R.recv)
    greeted = L.greet()
    R.await_in(*WEIGHTS_IN)
    pack_weights(L, R)
    R.await_in("tok", "cot")
    R.xall[L.z] = R.tok[...]
    R.cotall[L.z] = R.cot[...]
    greeted()

    moves = to_slab(L, R.pack, R.exch)
    xgen = gather_blocks(L, R.xall)
    step(xgen)
    wo = L.copy(R.opack.at[1 - L.c], R.exo, L.sibling)
    R.await_in("seg", "taps", "bias")
    setup(L, R)
    come(*moves)
    own_rows(L, R, R.exch, (LATE, EARLY), GW)
    late = together(*[gather_mixer(L, R, sub, *LATE) for sub in range(2)])
    step(late)
    come(wo)
    own_halves(L, R, R.opack, R.exo, OUT)
    R.await_in("w_fg", "w_fu", "w_fd")
    pack_ffn(L, R)
    fmoves = to_slab(L, R.fpack, R.fexch)
    do = L.copy(R.dpack.at[1 - L.c], R.dexo, L.sibling)
    step(late)
    rest = together(
        *[gather_mixer(L, R, sub, EARLY[0], EARLY[1] + OUT[1]) for sub in range(2)]
    )
    step(rest)
    cgen = gather_blocks(L, R.cotall)
    R.small[...] = jnp.zeros((8, CW), F32)
    R.gk[...] = jnp.zeros((LEN, 128), F32)
    R.gv[...] = jnp.zeros((LEN, 128), F32)
    R.state[0] = jnp.zeros((128, XW), F32)
    step(late)
    step(rest)
    come(do, *fmoves)
    own_rows(L, R, R.fexch, (FIN,), FW)
    own_halves(L, R, R.dpack, R.dexo, FOUT)
    fsent = []
    fgen = together(*[gather_mixer(L, R, sub, *FFN, fsent) for sub in range(2)])
    step(fgen)
    drain(late)
    drain(xgen)
    step(cgen)

    gains(R)
    norm_first(R)
    project_late(R)
    convolve(R)
    steps(R)
    step(rest, fgen)
    recurrence(R, 0, 2)
    drain(rest)
    project_early(R)
    R.await_in("cosr", "sinr", "perm5")
    rotated(R)
    attend(R, 0, 2)
    out_project(R, 0)
    branch = [to_owner(L, R, R.branch.at[h], h) for h in range(2)]
    step(branch[0])
    step(fgen)
    recurrence(R, 2, 4)
    attend(R, 2, 4)
    out_project(R, 1)
    step(branch[1])
    second = [gather_blocks(L, R.secall.at[h]) for h in range(2)]
    for h in range(2):
        drain(branch[h])
        middle_rows(L, R, h)
        step(second[h])
    drain(cgen, fgen)
    gsec = [to_owner(L, R, R.gsec.at[h], 2 + h) for h in range(2)]
    for h in range(2):
        drain(second[h])
        ffn(R, h)
        step(gsec[h])
    gball = [gather_blocks(L, R.gball.at[h]) for h in range(2)]
    drain(gsec[0])
    back_middle(L, R, 0)
    step(gball[0])
    ffn_out(R, L)
    for one in fsent:
        one.wait_send()
    ffn_grads(R)
    wgen = reduce_ffn(L, R)
    step(wgen)
    drain(gsec[1])
    back_middle(L, R, 1)
    step(gball[1])
    step(wgen)
    drain(gball[0])
    back_out(R, 0)
    back_attend(R, 0, 2)
    step(wgen)
    drain(gball[1])
    fout = reduce_blocks(L, R.fout, R.frecv)
    step(fout)
    back_out(R, 1)
    out_grad(R)
    ogen = reduce_outputs(L, R)
    step(ogen)
    back_gate(R)
    back_attend(R, 2, 4)
    back_rotated(R)
    step(ogen, wgen)
    early_grads(R)
    egen = reduce_inputs(L, R, EARLY, GW)
    step(egen)
    back_recurrence(R)
    step(egen, ogen, wgen)
    back_convolve(R)
    late_grads(R)
    lgen = reduce_inputs(L, R, LATE, 0)
    step(lgen)
    mgen = reduce_small(L, R)
    step(mgen)
    hgen = back_first(R, L)
    step(hgen)
    step(lgen, mgen)
    step(hgen)
    step(egen, ogen, wgen)
    step(hgen)
    step(lgen, mgen)
    step(hgen)
    step(egen, ogen, wgen)
    drain(fout)
    R.o_out[...] = R.fout[L.z]
    R.send_out("o_out")
    step(lgen, mgen)
    step(egen, ogen, wgen)
    drain(ogen, egen, wgen)
    step(lgen, mgen)
    drain(mgen)
    drain(hgen)
    R.o_tok[...] = R.gfirst[L.z]
    R.send_out("o_tok")
    drain(lgen)
    unpack_inputs(R)
    R.send_out("o_min", "o_bc", "o_misc", "o_q", "o_k", "o_v", "o_conv", "o_head")
    L.finish()
    R.finish_out()


INS = dict(
    w_min=((8, 3072), F32),
    w_bc=((8, 256), F32),
    w_step=((8, 24), F32),
    w_q=((8, 512), F32),
    w_k=((8, 128), F32),
    w_v=((8, 128), F32),
    w_mo=((12, D), F32),
    w_ao=((4, D), F32),
    tok=((ROWS, D), BF),
    cot=((ROWS, D), BF),
    w_fg=((8, 2048), F32),
    w_fu=((8, 2048), F32),
    w_fd=((16, D), F32),
    seg=((1, LEN), jnp.int32),
    taps=((4, 1792), F32),
    bias=((1, 1792), F32),
    cosr=((LEN, 128), F32),
    sinr=((LEN, 128), F32),
    perm5=((512, 512), BF),
)
WEIGHTS_IN = list(INS)[:8]
SCALARS = ("gain_in", "gain_mid", "step_bias", "decay_log", "skip_gain")
OUTS = dict(
    o_out=((ROWS, D), BF),
    o_tok=((ROWS, D), BF),
    o_min=((8, 3072), F32),
    o_bc=((8, 256), F32),
    o_misc=((8, 128), F32),
    o_q=((8, 512), F32),
    o_k=((8, 128), F32),
    o_v=((8, 128), F32),
    o_mo=((12, D), F32),
    o_ao=((4, D), F32),
    o_fg=((8, 2048), F32),
    o_fu=((8, 2048), F32),
    o_fd=((16, D), F32),
    o_conv=((8, 1792), F32),
    o_head=((8, 128), F32),
)
SCRATCH = dict(
    xall=((4, ROWS, D), BF),
    segc=((LEN, 128), F32),
    segr=((8, LEN), F32),
    cpar=((8, CW), F32),
    hpar=((8, 128), F32),
    misc=((8, 128), F32),
    pack=((4, 2, 8, 768), F32),
    exch=((4, 2, 8, 768), F32),
    opack=((2, 16, 512), F32),
    exo=((16, 512), F32),
    fpack=((4, 2, 8, FW), F32),
    fexch=((4, 2, 8, FW), F32),
    dpack=((2, 16, 512), F32),
    dexo=((16, 512), F32),
    win=((2, 2, 4, 4, 16, PK), BF),
    dwin=((2, 2, 4, 4, 16, FIN[0]), BF),
    cotall=((4, ROWS, D), BF),
    secall=((2, 4, 64, D), BF),
    hid=((LEN, FW), BF),
    gab=((LEN, 2 * FW), BF),
    gsec=((2, 4, 64, D), BF),
    fout=((4, ROWS, D), BF),
    gain=((8, D), F32),
    gcol=((1, 8, 128), F32),
    first=((LEN, D), BF),
    gate=((LEN, XW), F32),
    raw=((LEN, CW), BF),
    pq=((LEN, 128), F32),
    pkv=((LEN, 128), F32),
    pm=((LEN, 128), F32),
    pre=((LEN, CW), F32),
    mixed=((LEN, CW), F32),
    step=((LEN, 128), F32),
    run=((LEN, 128), F32),
    state=((5, 128, XW), F32),
    ssm=((LEN, XW), F32),
    q=((LEN, 128), BF),
    kk=((LEN, 128), BF),
    vv=((LEN, 128), BF),
    probs=((2, LEN, LEN), BF),
    left=((LEN, 512), BF),
    left_p=((LEN, 512), BF),
    branch=((2, 4, 64, D), BF),
    zrecv=((4, 3, 64, D), BF),
    frecv=((3, ROWS, D), BF),
    hrecv=((3, ROWS, D), BF),
    middle=((2, 64, D), F32),
    gmid=((2, 64, D), F32),
    gsum=((ROWS, D), F32),
    gball=((2, 4, 64, D), BF),
    gleft=((LEN, 512), F32),
    gq=((LEN, 128), F32),
    gk=((LEN, 128), F32),
    gv=((LEN, 128), F32),
    gstate=((128, XW), F32),
    hsum=((8, 128), F32),
    gmix=((LEN, CW), F32),
    gproj=((LEN, 4 * GW), BF),
    small=((8, CW), F32),
    factor=((4, 8, 128), F32),
    inlet_x=((LEN, XW), F32),
    tail_x=((LEN, XW), F32),
    factor_x=((4, 8, XW), F32),
    step_x=((LEN, XW), F32),
    mix=((4, HEADS, ROWS, ROWS), BF),
    weights=((4, HEADS, ROWS, ROWS), BF),
    gfirst=((4, ROWS, D), BF),
    wsib=((2, 4, 4, 16, PK), BF),
    smc=((2, 8, CW), F32),
    smx=((4, 8, CW), F32),
    smy=((4, 8, CW), F32),
    smz=((4, 8, CW), F32),
    fin=((4, 2, 8, 768), F32),
    rfin=((4, 2, 8, 768), F32),
    ofin=((2, 16, 512), F32),
    orfin=((16, 512), F32),
    ffin=((4, 2, 8, FW), F32),
    frfin=((4, 2, 8, FW), F32),
    dfin=((2, 16, 512), F32),
    drfin=((16, 512), F32),
)
COPIES = 250


def ring_buffers(parts, width, stages):
    shapes = {}
    for stage in range(stages):
        for n in range(3):
            shapes[(stage, n)] = ((parts,) + (4,) * stage + (16, width), BF)
    return shapes


MBUFS = ring_buffers(2, PK, 2)


def entry(*refs):
    refs = list(refs)
    take = lambda names: [(name, refs.pop(0)) for name in names]
    given, scalars, results = dict(take(INS)), take(SCALARS), dict(take(OUTS))
    inside = take(INS)
    R = types.SimpleNamespace(**dict(scalars + inside + take(OUTS) + take(SCRATCH)))
    bufs = dict(take(MBUFS))
    R.mbufs = [[bufs[key] for key in MBUFS if key[0] == stage] for stage in range(2)]
    R.send, R.recv, came, left = refs
    loads = {}
    for n, name in enumerate(INS):
        loads[name] = pltpu.make_async_copy(given[name], getattr(R, name), came.at[n])
        loads[name].start()
    stores = []

    def await_in(*names):
        for name in names:
            loads[name].wait()

    def send_out(*names):
        for name in names:
            n = len(stores)
            stores.append(pltpu.make_async_copy(getattr(R, name), results[name], left.at[n]))
            stores[-1].start()

    def finish_out():
        for one in stores:
            one.wait()

    R.await_in, R.send_out, R.finish_out = await_in, send_out, finish_out
    kernel(R)


def layer(*args):
    anywhere = pl.BlockSpec(memory_space=pl.ANY)
    smem = pl.BlockSpec(memory_space=pltpu.SMEM)
    shapes = [*INS.values(), *OUTS.values(), *SCRATCH.values(), *MBUFS.values()]
    scratch = [pltpu.VMEM(shape, kind) for shape, kind in shapes]
    scratch += [pltpu.SemaphoreType.DMA((n,)) for n in (COPIES, COPIES, len(INS), len(OUTS))]
    return pl.pallas_call(
        entry,
        out_shape=[jax.ShapeDtypeStruct(shape, kind) for shape, kind in OUTS.values()],
        in_specs=[anywhere] * len(INS) + [smem] * len(SCALARS),
        out_specs=[anywhere] * len(OUTS),
        scratch_shapes=scratch,
        compiler_params=pltpu.CompilerParams(
            collective_id=0, has_side_effects=True, vmem_limit_bytes=63 * 2**20
        ),
    )(*args)


SAME = [name for name in OUTS if name not in ("o_misc", "o_conv", "o_head")]
RESULTS = {name: OUTS[name] for name in SAME}
RESULTS.update(
    step=((8, 24), F32),
    taps=((4, 1792), F32),
    bias=((1, 1792), F32),
    gain_in=((1, 8), F32),
    gain_mid=((1, 8), F32),
    step_bias=((1, 24), F32),
    decay_log=((1, 24), F32),
    skip_gain=((1, 24), F32),
)


def deliver_kernel(*refs):
    given = dict(zip(OUTS, refs))
    result = dict(zip(RESULTS, refs[len(OUTS) :]))
    for name in SAME:
        result[name][...] = given[name][...]
    result["step"][...] = given["o_misc"][:, 0:24]
    result["taps"][...] = given["o_conv"][0:4, :]
    result["bias"][...] = given["o_conv"][4:5, :]
    head = given["o_head"]
    for row, name in enumerate(("step_bias", "decay_log", "skip_gain")):
        result[name][...] = head[row : row + 1, 0:24]
    result["gain_in"][...] = head[3:4, 0:8]
    result["gain_mid"][...] = head[4:5, 0:8]


def deliver(outs):
    vmem = pl.BlockSpec(memory_space=pltpu.VMEM)
    results = pl.pallas_call(
        deliver_kernel,
        out_shape=[jax.ShapeDtypeStruct(shape, kind) for shape, kind in RESULTS.values()],
        in_specs=[vmem] * len(OUTS),
        out_specs=[vmem] * len(RESULTS),
    )(*outs)
    return dict(zip(RESULTS, results))


def rotary_tables():
    lane = np.arange(128)
    power = (-2.0 * (lane % 32).astype(np.float32) / np.float32(64)).astype(np.float32)
    frequency = np.power(np.float32(ROPE), power).astype(np.float32)
    angles = np.arange(LEN, dtype=np.float32)[:, None] * frequency[None, :]
    sign = np.where(lane % 64 < 32, -1.0, 1.0)
    cosine = np.cos(angles.astype(np.float64)).astype(np.float32)
    sine = (np.sin(angles.astype(np.float64)) * sign).astype(np.float32)
    return cosine, sine


def out_order():
    n = np.arange(512)
    device = np.where(n < 384, n // 12, (n - 384) // 4)
    row = np.where(n < 384, n % 12, 12 + (n - 384) % 4)
    to = (device % 2) * 256 + (device // 2) * 16 + row
    table = np.zeros((512, 512), np.float32)
    table[n, to] = 1.0
    return table


def shards(
    tokens,
    segments,
    cotangent,
    gain_in,
    mamba_in,
    mamba_bc,
    mamba_step,
    in_query,
    in_key,
    in_value,
    mamba_out,
    attn_out,
    gain_mid,
    ffn_gate,
    ffn_up,
    ffn_down,
    conv_taps,
    conv_bias,
    step_bias,
    decay_log,
    skip_gain,
):
    cosine, sine = rotary_tables()
    outs = layer(
        mamba_in,
        mamba_bc,
        mamba_step,
        in_query,
        in_key,
        in_value,
        mamba_out,
        attn_out,
        tokens[0],
        cotangent[0],
        ffn_gate,
        ffn_up,
        ffn_down,
        segments,
        conv_taps,
        conv_bias[None],
        jnp.asarray(cosine),
        jnp.asarray(sine),
        jnp.asarray(out_order(), BF),
        gain_in,
        gain_mid,
        step_bias,
        decay_log,
        skip_gain,
    )
    r = deliver(outs)
    return (
        r["o_out"][None],
        r["o_tok"][None],
        r["gain_in"][0],
        r["o_min"],
        r["o_bc"],
        r["step"],
        r["o_q"],
        r["o_k"],
        r["o_v"],
        r["o_mo"],
        r["o_ao"],
        r["gain_mid"][0],
        r["o_fg"],
        r["o_fu"],
        r["o_fd"],
        r["taps"],
        r["bias"][0],
        r["step_bias"][0],
        r["decay_log"][0],
        r["skip_gain"][0],
    )


def solution(mesh):
    one = P(("ctx", "fsdp"))
    rows = P(("ctx", "fsdp"), None)
    block = P("fsdp", "ctx", None)
    return jax.shard_map(
        shards,
        mesh=mesh,
        in_specs=(block, P("fsdp", None), block, one)
        + (rows,) * 8
        + (one,)
        + (rows,) * 3
        + (P(),) * 5,
        out_specs=(block, block, one) + (rows,) * 8 + (one,) + (rows,) * 3 + (P(),) * 5,
        check_vma=False,
    )
```

time: 4220 us -> 146 us (0.03)
  waiting for transfers between devices: 3160 us -> 0 us
  blocking collectives: 672 us -> 0 us
  Pallas kernels: 0 us -> 142 us
  matrix products: 117 us -> 0 us
  local copies, waits for them, and re-layouts: 99.8 us -> 1.99 us
  starting transfers between devices: 91.6 us -> 0 us
  other arithmetic: 46.7 us -> 0.62 us
    reduce_scatter x6 -> x0, waiting for transfers between devices: 2940 us -> none  [the longest x1 647 us: shards(): lax.psum_scatter(weight_grad(hidden, grad_low), ('ctx', 'fsdp'), scatter_...]
    unnamed x2 -> x0, blocking collectives: 445 us -> none
    all_gather x9 -> x0, waiting for transfers between devices: 215 us -> none  [the longest x1 64.2 us: shards(): lax.all_gather(ffn_up.astype(jnp.bfloat16), ('ctx', 'fsdp'), axis=0, tile...]
    all_gather x7 -> x0, blocking collectives: 165 us -> none  [the longest x1 36.4 us: shards(): lax.all_gather(in_key.astype(jnp.bfloat16), ('ctx', 'fsdp'), axis=0, tile...]
    pallas_call x0 -> x2, Pallas kernels: none -> 142 us  [the longest x1 140 us: layer(): pl.pallas_call(entry, out_shape=[jax.ShapeDtypeStruct(shape, kind) for sh...]
    dot_general x50 -> x0, matrix products: 115 us -> none  [the longest x11 34 us: weight_grad(): lax.dot_general(input_rows, grad_rows, (((0,), (0,)), ((), ())), preferre...]
    unnamed x34 -> x0, starting transfers between devices: 88 us -> none
    unnamed x324 -> x2, local copies, waits for them, and re-layouts: 78.5 us -> 0.69 us
  transfers between devices with their start and end apart: 51 -> 0, of which waited for: 13 -> 0; matrix products, arithmetic and copies ran while one was open for 14% -> 0% of each run, Pallas kernels for 0% -> 0%
where the time goes in v1:
time: 146 us; the launch traced here: 145 us
  Pallas kernels  142 us (97%)
  local copies, waits for them, and re-layouts  1.99 us (1%)
    pallas_call x1, Pallas kernels, layer(): pl.pallas_call(entry, out_shape=[jax.ShapeDtypeStruct(shape, kind) for sh...  140 us

profile of v1, /device:TPU:1, one launch (start us, length us, event | category | flops | bytes accessed | tf_op | source)
XLA Modules:
  0.0 145.3 jit_solution(14120288804026159623)
XLA Ops:
  0.7 1.3 broadcast_in_dim.9.refs_15_
  2.0 139.8 %shard_map.383 = (bf16[128,1024]{1,0:T(8,128)(2,1)}, bf16[128,1024]{1,0:T(8,128)(2,1)}, f32[8,3072]{1,0:T(8,128)}, f32[8,256]{1,0:T(8,128)}, f32[8,128]{1,0:T(8,...) custom-call(f32[8,3072]{1,0:T(8,128)} %refs_0_.1, ...), custom_call_target="tpu_custom_call" | custom-call | tf_op jit(solution)/shard_map/pallas_call | solution.py:1377
  141.8 2.2 %shard_map.384 = (bf16[128,1024]{1,0:T(8,128)(2,1)}, bf16[128,1024]{1,0:T(8,128)(2,1)}, f32[8,3072]{1,0:T(8,128)}, f32[8,256]{1,0:T(8,128)}, f32[8,512]{1,0:T(8,...) custom-call(bf16[128,1024]{1,0:T(8,128)(2,1)} %get-tuple-element.55., ...), custom_call_target="tpu_custom_call" | custom-call | tf_op jit(solution)/shard_map/pallas_call | solution.py:1420
  144.0 0.0 copy-start
  144.0 0.7 copy-done
  144.7 0.6 reduce
Async XLA Ops:
  144.0 0.7 copy-start

commit v2 on v1

--- a/solution.py
+++ b/solution.py
@@ -421,9 +421,7 @@
     R.gproj[:, 1408:1536] = jnp.zeros((LEN, 128), BF)
 
 
-def back_recurrence(R):
-    R.gstate[...] = jnp.zeros((128, XW), F32)
-    R.hsum[...] = jnp.zeros((8, 128), F32)
+def back_recurrence(R, begin, end):
     low = lane_low((ROWS, 128))
     lane = iota((ROWS, 128), 1)
     sub = iota((ROWS, 128), 0)
@@ -505,7 +503,7 @@
         R.gstate[...] = R.factor_x[b, 0:1, :] * gstate + mm_tn(s.rd_low, flow_low)
         return carry
 
-    lax.fori_loop(0, 4, block, 0)
+    lax.fori_loop(begin, end, block, 0)
 
 
 def back_convolve(R):
@@ -811,19 +809,21 @@
     return L.copy(fin.at[1 - L.c], rfin, L.sibling)
 
 
-def reduce_inputs(L, R, kind, place):
-    yield from reduce_mixer(L, R, R.dwin, *kind)
-    moves = deal_rows(L, R.dwin, kind, GW, R.fin, R.rfin, place)
+def reduce_late(L, R):
+    yield from reduce_mixer(L, R, R.dwin, *LATE)
+    moves = deal_rows(L, R.dwin, LATE, GW, R.fin, R.rfin, 0)
     yield
     for one in moves:
         one.wait_recv()
 
 
-def reduce_outputs(L, R):
-    yield from reduce_mixer(L, R, R.dwin, *OUT)
-    move = deal_halves(L, R.dwin, OUT, R.ofin, R.orfin)
+def reduce_early(L, R):
+    yield from reduce_mixer(L, R, R.dwin, EARLY[0], EARLY[1] + OUT[1])
+    moves = deal_rows(L, R.dwin, EARLY, GW, R.fin, R.rfin, GW)
+    moves.append(deal_halves(L, R.dwin, OUT, R.ofin, R.orfin))
     yield
-    move.wait_recv()
+    for one in moves:
+        one.wait_recv()
     lo, hi = in_core_order(L, R.ofin[L.c], R.orfin[...])
     R.o_mo[:, 0:512] = lo[0:12, :]
     R.o_mo[:, 512:1024] = hi[0:12, :]
@@ -897,8 +897,8 @@
     cols = pl.ds(pl.multiple_of(XW * L.z, 128), XW)
     R.cpar[0:4, 0:384] = R.taps[:, cols]
     R.cpar[0:4, 384:640] = R.taps[:, 1536:1792]
-    R.cpar[4:5, 0:384] = R.bias[:, cols]
-    R.cpar[4:5, 384:640] = R.bias[:, 1536:1792]
+    R.cpar[4:5, 0:384] = R.bias[cols].reshape(1, 384)
+    R.cpar[4:5, 384:640] = R.bias[1536:1792].reshape(1, 256)
     lane = iota((1, XW), 1) // 64
     total = jnp.zeros((1, XW), F32)
     for h in range(HEADS):
@@ -1064,51 +1064,52 @@
     greeted()
 
     moves = to_slab(L, R.pack, R.exch)
-    xgen = gather_blocks(L, R.xall)
-    step(xgen)
     wo = L.copy(R.opack.at[1 - L.c], R.exo, L.sibling)
     R.await_in("seg", "taps", "bias")
     setup(L, R)
+    R.await_in("w_fg", "w_fu", "w_fd")
+    pack_ffn(L, R)
     come(*moves)
     own_rows(L, R, R.exch, (LATE, EARLY), GW)
     late = together(*[gather_mixer(L, R, sub, *LATE) for sub in range(2)])
     step(late)
+    xgen = gather_blocks(L, R.xall)
+    step(xgen)
+    fmoves = to_slab(L, R.fpack, R.fexch)
+    do = L.copy(R.dpack.at[1 - L.c], R.dexo, L.sibling)
     come(wo)
     own_halves(L, R, R.opack, R.exo, OUT)
-    R.await_in("w_fg", "w_fu", "w_fd")
-    pack_ffn(L, R)
-    fmoves = to_slab(L, R.fpack, R.fexch)
-    do = L.copy(R.dpack.at[1 - L.c], R.dexo, L.sibling)
     step(late)
-    rest = together(
+    early = together(
         *[gather_mixer(L, R, sub, EARLY[0], EARLY[1] + OUT[1]) for sub in range(2)]
     )
-    step(rest)
-    cgen = gather_blocks(L, R.cotall)
+    step(early)
     R.small[...] = jnp.zeros((8, CW), F32)
     R.gk[...] = jnp.zeros((LEN, 128), F32)
     R.gv[...] = jnp.zeros((LEN, 128), F32)
     R.state[0] = jnp.zeros((128, XW), F32)
+    R.gstate[...] = jnp.zeros((128, XW), F32)
+    R.hsum[...] = jnp.zeros((8, 128), F32)
     step(late)
-    step(rest)
+    step(early)
+    drain(late)
+    gains(R)
+    drain(xgen)
+    cgen = gather_blocks(L, R.cotall)
+    step(cgen)
+    norm_first(R)
+    project_late(R)
+    convolve(R)
     come(do, *fmoves)
     own_rows(L, R, R.fexch, (FIN,), FW)
     own_halves(L, R, R.dpack, R.dexo, FOUT)
     fsent = []
     fgen = together(*[gather_mixer(L, R, sub, *FFN, fsent) for sub in range(2)])
     step(fgen)
-    drain(late)
-    drain(xgen)
-    step(cgen)
-
-    gains(R)
-    norm_first(R)
-    project_late(R)
-    convolve(R)
     steps(R)
-    step(rest, fgen)
     recurrence(R, 0, 2)
-    drain(rest)
+    drain(early)
+    step(fgen)
     project_early(R)
     R.await_in("cosr", "sinr", "perm5")
     rotated(R)
@@ -1116,11 +1117,11 @@
     out_project(R, 0)
     branch = [to_owner(L, R, R.branch.at[h], h) for h in range(2)]
     step(branch[0])
-    step(fgen)
     recurrence(R, 2, 4)
     attend(R, 2, 4)
     out_project(R, 1)
     step(branch[1])
+    step(fgen)
     second = [gather_blocks(L, R.secall.at[h]) for h in range(2)]
     for h in range(2):
         drain(branch[h])
@@ -1133,12 +1134,12 @@
         ffn(R, h)
         step(gsec[h])
     gball = [gather_blocks(L, R.gball.at[h]) for h in range(2)]
+    for one in fsent:
+        one.wait_send()
+    ffn_out(R, L)
     drain(gsec[0])
     back_middle(L, R, 0)
     step(gball[0])
-    ffn_out(R, L)
-    for one in fsent:
-        one.wait_send()
     ffn_grads(R)
     wgen = reduce_ffn(L, R)
     step(wgen)
@@ -1149,26 +1150,26 @@
     drain(gball[0])
     back_out(R, 0)
     back_attend(R, 0, 2)
-    step(wgen)
     drain(gball[1])
     fout = reduce_blocks(L, R.fout, R.frecv)
     step(fout)
     back_out(R, 1)
-    out_grad(R)
-    ogen = reduce_outputs(L, R)
-    step(ogen)
     back_gate(R)
     back_attend(R, 2, 4)
     back_rotated(R)
-    step(ogen, wgen)
+    out_grad(R)
     early_grads(R)
-    egen = reduce_inputs(L, R, EARLY, GW)
+    egen = reduce_early(L, R)
     step(egen)
-    back_recurrence(R)
-    step(egen, ogen, wgen)
+    step(wgen)
+    back_recurrence(R, 0, 2)
+    step(egen)
+    step(wgen)
+    back_recurrence(R, 2, 4)
     back_convolve(R)
+    step(wgen)
     late_grads(R)
-    lgen = reduce_inputs(L, R, LATE, 0)
+    lgen = reduce_late(L, R)
     step(lgen)
     mgen = reduce_small(L, R)
     step(mgen)
@@ -1176,18 +1177,18 @@
     step(hgen)
     step(lgen, mgen)
     step(hgen)
-    step(egen, ogen, wgen)
+    step(egen)
     step(hgen)
-    step(lgen, mgen)
+    step(mgen)
     step(hgen)
-    step(egen, ogen, wgen)
-    drain(fout)
+    step(lgen)
+    step(egen)
+    step(mgen)
+    drain(wgen, fout)
     R.o_out[...] = R.fout[L.z]
     R.send_out("o_out")
-    step(lgen, mgen)
-    step(egen, ogen, wgen)
-    drain(ogen, egen, wgen)
-    step(lgen, mgen)
+    step(lgen)
+    drain(egen)
     drain(mgen)
     drain(hgen)
     R.o_tok[...] = R.gfirst[L.z]
@@ -1215,7 +1216,7 @@
     w_fd=((16, D), F32),
     seg=((1, LEN), jnp.int32),
     taps=((4, 1792), F32),
-    bias=((1, 1792), F32),
+    bias=((1792,), F32),
     cosr=((LEN, 128), F32),
     sinr=((LEN, 128), F32),
     perm5=((512, 512), BF),
@@ -1391,12 +1392,12 @@
 RESULTS.update(
     step=((8, 24), F32),
     taps=((4, 1792), F32),
-    bias=((1, 1792), F32),
-    gain_in=((1, 8), F32),
-    gain_mid=((1, 8), F32),
-    step_bias=((1, 24), F32),
-    decay_log=((1, 24), F32),
-    skip_gain=((1, 24), F32),
+    bias=((1792,), F32),
+    gain_in=((8,), F32),
+    gain_mid=((8,), F32),
+    step_bias=((24,), F32),
+    decay_log=((24,), F32),
+    skip_gain=((24,), F32),
 )
 
 
@@ -1407,12 +1408,12 @@
         result[name][...] = given[name][...]
     result["step"][...] = given["o_misc"][:, 0:24]
     result["taps"][...] = given["o_conv"][0:4, :]
-    result["bias"][...] = given["o_conv"][4:5, :]
+    result["bias"][...] = given["o_conv"][4, :]
     head = given["o_head"]
     for row, name in enumerate(("step_bias", "decay_log", "skip_gain")):
-        result[name][...] = head[row : row + 1, 0:24]
-    result["gain_in"][...] = head[3:4, 0:8]
-    result["gain_mid"][...] = head[4:5, 0:8]
+        result[name][...] = head[row, 0:24]
+    result["gain_in"][...] = head[3, 0:8]
+    result["gain_mid"][...] = head[4, 0:8]
 
 
 def deliver(outs):
@@ -1487,7 +1488,7 @@
         ffn_down,
         segments,
         conv_taps,
-        conv_bias[None],
+        conv_bias,
         jnp.asarray(cosine),
         jnp.asarray(sine),
         jnp.asarray(out_order(), BF),
@@ -1501,7 +1502,7 @@
     return (
         r["o_out"][None],
         r["o_tok"][None],
-        r["gain_in"][0],
+        r["gain_in"],
         r["o_min"],
         r["o_bc"],
         r["step"],
@@ -1510,15 +1511,15 @@
         r["o_v"],
         r["o_mo"],
         r["o_ao"],
-        r["gain_mid"][0],
+        r["gain_mid"],
         r["o_fg"],
         r["o_fu"],
         r["o_fd"],
         r["taps"],
-        r["bias"][0],
-        r["step_bias"][0],
-        r["decay_log"][0],
-        r["skip_gain"][0],
+        r["bias"],
+        r["step_bias"],
+        r["decay_log"],
+        r["skip_gain"],
     )
 
 

time: 146 us -> 132 us (0.904)
  Pallas kernels: 142 us -> 131 us
  local copies, waits for them, and re-layouts: 1.99 us -> 0 us
    pallas_call x1, Pallas kernels: 140 us -> 129 us  [layer(): pl.pallas_call(entry, out_shape=[jax.ShapeDtypeStruct(shape, kind) for sh...]
where the time goes in v2:
time: 132 us
  Pallas kernels  131 us (99%)
    pallas_call x1, Pallas kernels, layer(): pl.pallas_call(entry, out_shape=[jax.ShapeDtypeStruct(shape, kind) for sh...  129 us

profile of v2, /device:TPU:1, one launch (start us, length us, event | category | flops | bytes accessed | tf_op | source)
XLA Modules:
  0.0 132.1 jit_solution(1585075845108659337)
XLA Ops:
  0.7 129.0 %shard_map.383 = (bf16[128,1024]{1,0:T(8,128)(2,1)}, bf16[128,1024]{1,0:T(8,128)(2,1)}, f32[8,3072]{1,0:T(8,128)}, f32[8,256]{1,0:T(8,128)}, f32[8,128]{1,0:T(8,...) custom-call(f32[8,3072]{1,0:T(8,128)} %refs_0_.1, ...), custom_call_target="tpu_custom_call" | custom-call | tf_op jit(solution)/shard_map/pallas_call | solution.py:1378
  129.7 2.2 %shard_map.384 = (bf16[128,1024]{1,0:T(8,128)(2,1)}, bf16[128,1024]{1,0:T(8,128)(2,1)}, f32[8,3072]{1,0:T(8,128)}, f32[8,256]{1,0:T(8,128)}, f32[8,512]{1,0:T(8,...) custom-call(bf16[128,1024]{1,0:T(8,128)(2,1)} %get-tuple-element.55., ...), custom_call_target="tpu_custom_call" | custom-call | tf_op jit(solution)/shard_map/pallas_call | solution.py:1421

commit v3 on v2

--- a/solution.py
+++ b/solution.py
@@ -11,7 +11,6 @@
 BF = jnp.bfloat16
 F32 = jnp.float32
 MESH = pl.DeviceIdType.MESH
-HI = lax.Precision.HIGHEST
 EPS = 1e-06
 ROPE = 100000000000.0
 
@@ -38,18 +37,12 @@
     return lax.dot_general(a, b, (((0,), (0,)), ((), ())), preferred_element_type=F32)
 
 
-def mm_exact(a, b):
-    return lax.dot_general(
-        a, b, (((1,), (0,)), ((), ())), precision=HI, preferred_element_type=F32
-    )
-
-
 def iota(shape, dim):
     return lax.broadcasted_iota(jnp.int32, shape, dim)
 
 
 def lane_low(shape):
-    return iota(shape, 1) % 128 < 64
+    return iota(shape, 1) & 64 == 0
 
 
 def roll(v, shift, axis):
@@ -59,7 +52,7 @@
 
 def swap_halves(v):
     lanes = v.shape[1]
-    first = iota(v.shape, 1) % 64 < 32
+    first = iota(v.shape, 1) & 32 == 0
     return jnp.where(first, roll(v, lanes - 32, 1), roll(v, 32, 1))
 
 
@@ -94,7 +87,7 @@
 
 
 def sum_heads(v):
-    pick = (iota((XW, 128), 0) // 64 == iota((XW, 128), 1)).astype(BF)
+    pick = (iota((XW, 128), 0) >> 6 == iota((XW, 128), 1)).astype(BF)
     return mm_terms(v, pick, 2)
 
 
@@ -747,20 +740,29 @@
     return axis, slot
 
 
-def gather_mixer(L, R, sub, lo, width, log=None):
+def gather_near(L, R, sub, lo, width, log=None):
+    axis, slot = mixer_slot(L, R.win, sub, 0, lo, width)
+    return gather(L, axis, slot, None, log)
+
+
+def gather_far(L, R, sub, lo, width, log=None):
+    axis, slot = mixer_slot(L, R.win, sub, 1, lo, width)
     sent = []
-    for stage in range(2):
-        axis, slot = mixer_slot(L, R.win, sub, stage, lo, width)
-
-        def arrived(j, slot=slot):
-            sent.append(L.copy(slot(j), slot(j), L.sibling))
-
-        yield from gather(L, axis, slot, arrived if stage == 1 else None, log)
+
+    def arrived(j):
+        sent.append(L.copy(slot(j), slot(j), L.sibling))
+
+    yield from gather(L, axis, slot, arrived, log)
     if log is not None:
         log.extend(sent)
     yield
     for one in sent:
         one.wait_recv()
+
+
+def gather_mixer(L, R, sub, lo, width, log=None):
+    yield from gather_near(L, R, sub, lo, width, log)
+    yield from gather_far(L, R, sub, lo, width, log)
 
 
 def reduce_mixer(L, R, buf, lo, width):
@@ -842,9 +844,9 @@
     lo, hi = in_core_order(L, R.dfin[L.c], R.drfin[...])
     R.o_fd[:, 0:512] = lo
     R.o_fd[:, 512:1024] = hi
-    turn = (iota((FW, FW), 1) == deal(iota((FW, FW), 0))).astype(F32)
+    turn = (iota((FW, FW), 1) == deal(iota((FW, 1), 0))).astype(BF)
     rows = [R.frfin[j, core] for core in range(2) for j in range(4)]
-    out = mm_exact(jnp.concatenate(rows, axis=0), turn)
+    out = mm_terms(jnp.concatenate(rows, axis=0), turn, 3)
     for j in range(4):
         R.o_fg[:, FW * j : FW * j + FW] = out[8 * j : 8 * j + 8, :]
         R.o_fu[:, FW * j : FW * j + FW] = out[32 + 8 * j : 40 + 8 * j, :]
@@ -899,7 +901,7 @@
     R.cpar[0:4, 384:640] = R.taps[:, 1536:1792]
     R.cpar[4:5, 0:384] = R.bias[cols].reshape(1, 384)
     R.cpar[4:5, 384:640] = R.bias[1536:1792].reshape(1, 256)
-    lane = iota((1, XW), 1) // 64
+    lane = iota((1, XW), 1) >> 6
     total = jnp.zeros((1, XW), F32)
     for h in range(HEADS):
         total = jnp.where(lane == h, R.skip_gain[first + h], total)
@@ -941,11 +943,11 @@
 
 
 def deal(n):
-    return 32 * ((n % 256) // 16) + 16 * (n // 256) + n % 16
+    return 32 * ((n & 255) >> 4) + 16 * (n >> 8) + (n & 15)
 
 
 def pack_ffn(L, R):
-    turn = (iota((FW, FW), 0) == deal(iota((FW, FW), 1))).astype(BF)
+    turn = (iota((FW, FW), 0) == deal(iota((1, FW), 1))).astype(BF)
     rows = [ref[:, FW * j : FW * j + FW] for ref in (R.w_fg, R.w_fu) for j in range(4)]
     out = mm(jnp.concatenate(rows, axis=0).astype(BF), turn)
     for j in range(4):
@@ -967,31 +969,40 @@
     return total / gain.astype(BF).astype(F32)
 
 
-def unpack_inputs(R):
+def unpack_early(R):
+    low = lane_low((8, 128))
+    for j in range(4):
+        R.o_min[:, 384 * j : 384 * j + 384] = R.rfin[j, 0, :, 384:768]
+        R.o_q[:, 128 * j : 128 * j + 128] = R.rfin[j, 1, :, 384:512]
+    kv0 = R.rfin[0, 1, :, 512:640] + R.rfin[1, 1, :, 512:640]
+    kv1 = R.rfin[2, 1, :, 512:640] + R.rfin[3, 1, :, 512:640]
+    R.o_k[...] = jnp.where(low, kv0, roll(kv1, 64, 1))
+    R.o_v[...] = jnp.where(low, roll(kv0, 64, 1), kv1)
+    pairs = [(R.w_min.at[:, 0:1536], R.o_min.at[:, 0:1536])]
+    pairs += [(R.w_q, R.o_q), (R.w_k, R.o_k), (R.w_v, R.o_v)]
+    R.gcol[1] = gain_column(pairs, R.gain_in)
+    R.send_out("o_q", "o_k", "o_v")
+
+
+def unpack_late(R):
     lane = iota((8, 128), 1)
-    low = lane_low((8, 128))
     misc = jnp.zeros((8, 128), F32)
     for j in range(4):
-        R.o_min[:, 384 * j : 384 * j + 384] = R.rfin[j, 0, :, 384:768]
         R.o_min[:, 1536 + 384 * j : 1920 + 384 * j] = R.rfin[j, 0, :, 0:384]
-        R.o_q[:, 128 * j : 128 * j + 128] = R.rfin[j, 1, :, 384:512]
-        part = R.rfin[j, 1, :, 256:384]
-        own = jnp.where(lane < HEADS, part, 0.0)
+        own = jnp.where(lane < HEADS, R.rfin[j, 1, :, 256:384], 0.0)
         misc = misc + (own if j == 0 else roll(own, HEADS * j, 1))
     R.o_misc[...] = misc
     R.o_bc[...] = (R.rfin[0, 1, :, 0:256] + R.rfin[1, 1, :, 0:256]) + (
         R.rfin[2, 1, :, 0:256] + R.rfin[3, 1, :, 0:256]
     )
-    kv0 = R.rfin[0, 1, :, 512:640] + R.rfin[1, 1, :, 512:640]
-    kv1 = R.rfin[2, 1, :, 512:640] + R.rfin[3, 1, :, 512:640]
-    R.o_k[...] = jnp.where(low, kv0, roll(kv1, 64, 1))
-    R.o_v[...] = jnp.where(low, roll(kv0, 64, 1), kv1)
-    pairs = [(R.w_min, R.o_min), (R.w_bc, R.o_bc), (R.w_step, R.o_misc.at[:, 0:24])]
-    pairs += [(R.w_q, R.o_q), (R.w_k, R.o_k), (R.w_v, R.o_v)]
-    first = gain_column(pairs, R.gain_in)
+    R.send_out("o_min", "o_bc", "o_misc")
+    pairs = [(R.w_min.at[:, 1536:3072], R.o_min.at[:, 1536:3072])]
+    pairs += [(R.w_bc, R.o_bc), (R.w_step, R.o_misc.at[:, 0:24])]
+    first = R.gcol[1] + gain_column(pairs, R.gain_in)
     both = jnp.where(iota((8, 128), 1) == 0, first, R.gcol[0])
     turned = jnp.concatenate([both, jnp.zeros((120, 128), F32)], axis=0).T
     R.o_head[3:5, :] = turned[0:2, :]
+    R.send_out("o_head")
 
 
 def in_core_order(L, mine, other):
@@ -1069,21 +1080,24 @@
     setup(L, R)
     R.await_in("w_fg", "w_fu", "w_fd")
     pack_ffn(L, R)
+    come(wo)
+    own_halves(L, R, R.opack, R.exo, OUT)
     come(*moves)
     own_rows(L, R, R.exch, (LATE, EARLY), GW)
-    late = together(*[gather_mixer(L, R, sub, *LATE) for sub in range(2)])
-    step(late)
+    near = together(*[gather_near(L, R, sub, 0, FIN[0]) for sub in range(2)])
+    step(near)
     xgen = gather_blocks(L, R.xall)
     step(xgen)
     fmoves = to_slab(L, R.fpack, R.fexch)
     do = L.copy(R.dpack.at[1 - L.c], R.dexo, L.sibling)
-    come(wo)
-    own_halves(L, R, R.opack, R.exo, OUT)
+    drain(near)
+    late, early, out = [
+        together(*[gather_far(L, R, sub, *kind) for sub in range(2)])
+        for kind in (LATE, EARLY, OUT)
+    ]
     step(late)
-    early = together(
-        *[gather_mixer(L, R, sub, EARLY[0], EARLY[1] + OUT[1]) for sub in range(2)]
-    )
     step(early)
+    step(out)
     R.small[...] = jnp.zeros((8, CW), F32)
     R.gk[...] = jnp.zeros((LEN, 128), F32)
     R.gv[...] = jnp.zeros((LEN, 128), F32)
@@ -1091,7 +1105,6 @@
     R.gstate[...] = jnp.zeros((128, XW), F32)
     R.hsum[...] = jnp.zeros((8, 128), F32)
     step(late)
-    step(early)
     drain(late)
     gains(R)
     drain(xgen)
@@ -1099,7 +1112,9 @@
     step(cgen)
     norm_first(R)
     project_late(R)
+    step(early)
     convolve(R)
+    step(out)
     come(do, *fmoves)
     own_rows(L, R, R.fexch, (FIN,), FW)
     own_halves(L, R, R.dpack, R.dexo, FOUT)
@@ -1109,11 +1124,12 @@
     steps(R)
     recurrence(R, 0, 2)
     drain(early)
-    step(fgen)
     project_early(R)
     R.await_in("cosr", "sinr", "perm5")
     rotated(R)
     attend(R, 0, 2)
+    step(fgen)
+    drain(out)
     out_project(R, 0)
     branch = [to_owner(L, R, R.branch.at[h], h) for h in range(2)]
     step(branch[0])
@@ -1121,12 +1137,12 @@
     attend(R, 2, 4)
     out_project(R, 1)
     step(branch[1])
-    step(fgen)
     second = [gather_blocks(L, R.secall.at[h]) for h in range(2)]
     for h in range(2):
         drain(branch[h])
         middle_rows(L, R, h)
         step(second[h])
+        step(fgen)
     drain(cgen, fgen)
     gsec = [to_owner(L, R, R.gsec.at[h], 2 + h) for h in range(2)]
     for h in range(2):
@@ -1157,17 +1173,16 @@
     back_gate(R)
     back_attend(R, 2, 4)
     back_rotated(R)
+    step(wgen)
     out_grad(R)
     early_grads(R)
     egen = reduce_early(L, R)
     step(egen)
-    step(wgen)
     back_recurrence(R, 0, 2)
     step(egen)
     step(wgen)
     back_recurrence(R, 2, 4)
     back_convolve(R)
-    step(wgen)
     late_grads(R)
     lgen = reduce_late(L, R)
     step(lgen)
@@ -1177,25 +1192,26 @@
     step(hgen)
     step(lgen, mgen)
     step(hgen)
-    step(egen)
+    step(hgen)
     step(hgen)
     step(mgen)
-    step(hgen)
+    step(egen)
     step(lgen)
+    step(mgen)
     step(egen)
-    step(mgen)
+    step(lgen)
     drain(wgen, fout)
     R.o_out[...] = R.fout[L.z]
     R.send_out("o_out")
-    step(lgen)
     drain(egen)
+    unpack_early(R)
     drain(mgen)
+    R.send_out("o_conv")
     drain(hgen)
     R.o_tok[...] = R.gfirst[L.z]
     R.send_out("o_tok")
     drain(lgen)
-    unpack_inputs(R)
-    R.send_out("o_min", "o_bc", "o_misc", "o_q", "o_k", "o_v", "o_conv", "o_head")
+    unpack_late(R)
     L.finish()
     R.finish_out()
 
@@ -1264,7 +1280,7 @@
     gsec=((2, 4, 64, D), BF),
     fout=((4, ROWS, D), BF),
     gain=((8, D), F32),
-    gcol=((1, 8, 128), F32),
+    gcol=((2, 8, 128), F32),
     first=((LEN, D), BF),
     gate=((LEN, XW), F32),
     raw=((LEN, CW), BF),

time: 132 us -> 128 us (0.970)
  Pallas kernels: 131 us -> 127 us
    pallas_call x1, Pallas kernels: 129 us -> 125 us  [layer(): pl.pallas_call(entry, out_shape=[jax.ShapeDtypeStruct(shape, kind) for sh...]
where the time goes in v3:
time: 128 us
  Pallas kernels  127 us (99%)
    pallas_call x1, Pallas kernels, layer(): pl.pallas_call(entry, out_shape=[jax.ShapeDtypeStruct(shape, kind) for sh...  125 us

profile of v3, /device:TPU:1, one launch (start us, length us, event | category | flops | bytes accessed | tf_op | source)
XLA Modules:
  0.0 128.1 jit_solution(18440157581860554968)
XLA Ops:
  0.7 125.1 %shard_map.383 = (bf16[128,1024]{1,0:T(8,128)(2,1)}, bf16[128,1024]{1,0:T(8,128)(2,1)}, f32[8,3072]{1,0:T(8,128)}, f32[8,256]{1,0:T(8,128)}, f32[8,128]{1,0:T(8,...) custom-call(f32[8,3072]{1,0:T(8,128)} %refs_0_.1, ...), custom_call_target="tpu_custom_call" | custom-call | tf_op jit(solution)/shard_map/pallas_call | solution.py:1394
  125.7 2.2 %shard_map.384 = (bf16[128,1024]{1,0:T(8,128)(2,1)}, bf16[128,1024]{1,0:T(8,128)(2,1)}, f32[8,3072]{1,0:T(8,128)}, f32[8,256]{1,0:T(8,128)}, f32[8,512]{1,0:T(8,...) custom-call(bf16[128,1024]{1,0:T(8,128)(2,1)} %get-tuple-element.55., ...), custom_call_target="tpu_custom_call" | custom-call | tf_op jit(solution)/shard_map/pallas_call | solution.py:1437

commit v4 on v3

--- a/solution.py
+++ b/solution.py
@@ -569,8 +569,8 @@
             put_grad(R, core, EARLY, k, out[:, GW * core : GW * core + GW])
 
 
-def late_grads(R):
-    for k in range(4):
+def late_grads(R, sub):
+    for k in (2 * sub, 2 * sub + 1):
         out = mm_tn(R.first[:, 256 * k : 256 * k + 256], R.gproj[:, 0:768])
         for core in range(2):
             put_grad(R, core, LATE, k, out[:, GW * core : GW * core + GW])
@@ -692,7 +692,7 @@
             dst[where] = total.astype(BF)
             return carry
 
-        lax.fori_loop(0, count, body, 0)
+        lax.fori_loop(0, count, body, 0, unroll=min(count, 4))
 
     return add
 
@@ -765,9 +765,11 @@
     yield from gather_far(L, R, sub, lo, width, log)
 
 
-def reduce_mixer(L, R, buf, lo, width):
+def reduce_mixer(L, R, buf, lo, width, fill=None):
     moves = []
     for sub in range(2):
+        if fill:
+            fill(R, sub)
         theirs = columns(buf.at[1 - L.c, sub], 2, lo, width)
         moves.append(L.copy(theirs, columns(R.wsib.at[sub], 2, lo, width), L.sibling))
     yield
@@ -812,7 +814,7 @@
 
 
 def reduce_late(L, R):
-    yield from reduce_mixer(L, R, R.dwin, *LATE)
+    yield from reduce_mixer(L, R, R.dwin, *LATE, fill=late_grads)
     moves = deal_rows(L, R.dwin, LATE, GW, R.fin, R.rfin, 0)
     yield
     for one in moves:
@@ -1183,7 +1185,6 @@
     step(wgen)
     back_recurrence(R, 2, 4)
     back_convolve(R)
-    late_grads(R)
     lgen = reduce_late(L, R)
     step(lgen)
     mgen = reduce_small(L, R)

time: 128 us -> 127 us (level)
  no operation moved by 1% of the time
where the time goes in v4:
time: 127 us
  Pallas kernels  126 us (99%)
    pallas_call x1, Pallas kernels, layer(): pl.pallas_call(entry, out_shape=[jax.ShapeDtypeStruct(shape, kind) for sh...  124 us

profile of v4, /device:TPU:1, one launch (start us, length us, event | category | flops | bytes accessed | tf_op | source)
XLA Modules:
  0.0 127.3 jit_solution(10994573480541268812)
XLA Ops:
  0.7 124.2 %shard_map.383 = (bf16[128,1024]{1,0:T(8,128)(2,1)}, bf16[128,1024]{1,0:T(8,128)(2,1)}, f32[8,3072]{1,0:T(8,128)}, f32[8,256]{1,0:T(8,128)}, f32[8,128]{1,0:T(8,...) custom-call(f32[8,3072]{1,0:T(8,128)} %refs_0_.1, ...), custom_call_target="tpu_custom_call" | custom-call | tf_op jit(solution)/shard_map/pallas_call | solution.py:1395
  124.9 2.2 %shard_map.384 = (bf16[128,1024]{1,0:T(8,128)(2,1)}, bf16[128,1024]{1,0:T(8,128)(2,1)}, f32[8,3072]{1,0:T(8,128)}, f32[8,256]{1,0:T(8,128)}, f32[8,512]{1,0:T(8,...) custom-call(bf16[128,1024]{1,0:T(8,128)(2,1)} %get-tuple-element.55., ...), custom_call_target="tpu_custom_call" | custom-call | tf_op jit(solution)/shard_map/pallas_call | solution.py:1438
